TPU v7x, 32 devices: a whole 2x2x4 slice. The times are simulated.
32 devices in a mesh: section: 4 (over y, x), dp: 8 (over z, core).
Axes of the slice: x: 2, y: 2, z: 4, core: 2. Of those that a mesh axis runs over, the one named last changes fastest.
Arguments:
- boundary: bfloat16 [4, 8192, 768], P('section', 'dp'), may hold values from -6 to 6
- bucket_ids: int32 [2, 16, 4], P(None, 'dp'), may hold values from 0 to 3, as said below
- w_in: bfloat16 [2, 768, 3072], P(None, 'dp'), may hold values from -0.21875 to 0.21875
- b_in: float32 [2, 3072], replicated, may hold values from -3 to 3
- w_out: bfloat16 [2, 3072, 768], P(None, 'dp'), may hold values from -0.109375 to 0.109375
- b_out: float32 [2, 768], replicated, may hold values from -3 to 3
- gain_one: float32 [2, 768], replicated, may hold values from 0.5 to 1.5
- shift_one: float32 [2, 768], replicated, may hold values from -3 to 3
- gain_two: float32 [2, 768], replicated, may hold values from 0.5 to 1.5
- shift_two: float32 [2, 768], replicated, may hold values from -3 to 3
Outputs:
- result: float32 [4, 8192, 768], P('section', 'dp')
- grad_w_in: float32 [2, 768, 3072], P(None, 'dp')
- grad_b_in: float32 [2, 3072], P(None, 'dp')
- grad_w_out: float32 [2, 3072, 768], P(None, 'dp')
- grad_b_out: float32 [2, 768], P(None, 'dp')
- grad_gain_one: float32 [2, 768], P(None, 'dp')
- grad_shift_one: float32 [2, 768], P(None, 'dp')
- grad_gain_two: float32 [2, 768], P(None, 'dp')
- grad_shift_two: float32 [2, 768], P(None, 'dp')
Inputs may be any that keep to these rules, and one draw needn't show every extreme that they name: `bucket_ids`: each row lists the buckets of the sequences packed into one block of 512 tokens in order; bucket k holds sequences of 128 * 2**k tokens, 3 marks an empty slot; the used slots come first and their lengths add up to 512 exactly.
All inputs are finite; a program needn't handle non-finite values.
Results may differ from a plain program's by a relative error of at most 0.014.
Values may be sent and summed in bfloat16 or wider, within the bound.
No kernel may reach another device: no remote copies, remote signals or barrier semaphores. Data moves between devices by JAX's collectives and lax.ppermute only.
A program may use at most 256 MiB of HBM per device.

v0:
```python
from functools import partial
import math

import jax
import jax.numpy as jnp
from jax import lax
from jax.sharding import PartitionSpec as P


def partner(value, axis, apart):
    mask = 2**apart
    pairs = [(source, source ^ mask) for source in range(lax.axis_size(axis))]
    return lax.ppermute(value, axis, pairs)


def layer_norm(values, gain, shift):
    center = jnp.mean(values, axis=-1, keepdims=True)
    offsets = values - center
    spread = jnp.mean(offsets * offsets, axis=-1, keepdims=True)
    return offsets * lax.rsqrt(spread + 1e-05) * gain + shift


def hidden_tables(feat_width):
    positions = jnp.arange(feat_width, dtype=jnp.int32)
    phase_mod = positions[:, None] * positions[None, :] % feat_width
    angles = phase_mod.astype(jnp.float32) * (2.0 * math.pi) / feat_width
    scaling = 1.0 / math.sqrt(feat_width)
    return (
        (jnp.cos(angles) * scaling).astype(jnp.bfloat16),
        (jnp.sin(angles) * scaling).astype(jnp.bfloat16),
    )


def block_tables(bucket_row, slab_len, base_len):
    lengths = (
        base_len * (bucket_row == 0).astype(jnp.int32)
        + 2 * base_len * (bucket_row == 1).astype(jnp.int32)
        + 4 * base_len * (bucket_row == 2).astype(jnp.int32)
    )
    ends_at = jnp.cumsum(lengths)
    starts_at = ends_at - lengths
    positions = jnp.arange(slab_len, dtype=jnp.int32)
    segment = jnp.sum((positions[:, None] >= ends_at[None, :]).astype(jnp.int32), axis=1)
    one_hot = (
        segment[:, None] == jnp.arange(bucket_row.shape[0], dtype=jnp.int32)[None, :]
    ).astype(jnp.int32)
    row_start = jnp.sum(one_hot * starts_at[None, :], axis=1)
    row_length = jnp.sum(one_hot * lengths[None, :], axis=1)
    local_pos = positions - row_start
    same_seq = segment[:, None] == segment[None, :]
    phase_mod = local_pos[:, None] * local_pos[None, :] % row_length[:, None]
    angles = (
        phase_mod.astype(jnp.float32) * (2.0 * math.pi) / row_length[:, None].astype(jnp.float32)
    )
    scaling = lax.rsqrt(row_length.astype(jnp.float32))[:, None]
    cos_table = jnp.where(same_seq, jnp.cos(angles) * scaling, 0.0)
    sin_table = jnp.where(same_seq, jnp.sin(angles) * scaling, 0.0)
    return (cos_table.astype(jnp.bfloat16), sin_table.astype(jnp.bfloat16))


def contract_rows(left, right):
    return lax.dot_general(
        left, right, (((0,), (0,)), ((), ())), preferred_element_type=jnp.float32
    )


def contract_cols(left, right):
    return lax.dot_general(
        left, right, (((1,), (1,)), ((), ())), preferred_element_type=jnp.float32
    )


def forward_layer(layer_input, hid_cos, hid_sin, seq_cos, seq_sin, weights):
    w_first, b_first, w_second, b_second, gain_first, shift_first, gain_second, shift_second = (
        weights
    )
    real_part = jnp.dot(layer_input, hid_cos, preferred_element_type=jnp.float32).astype(
        jnp.bfloat16
    )
    imag_part = jnp.dot(layer_input, hid_sin, preferred_element_type=jnp.float32).astype(
        jnp.bfloat16
    )
    mixed = jnp.dot(seq_cos, real_part, preferred_element_type=jnp.float32) - jnp.dot(
        seq_sin, imag_part, preferred_element_type=jnp.float32
    )
    summed = layer_input.astype(jnp.float32) + mixed
    normed = layer_norm(summed, gain_first, shift_first)
    pre_act = (
        jnp.dot(normed.astype(jnp.bfloat16), w_first, preferred_element_type=jnp.float32) + b_first
    )
    hidden = jax.nn.gelu(pre_act, approximate=True).astype(jnp.bfloat16)
    second_sum = normed + (jnp.dot(hidden, w_second, preferred_element_type=jnp.float32) + b_second)
    out_rows = layer_norm(second_sum, gain_second, shift_second)
    return (out_rows, (summed, normed, pre_act, hidden, second_sum))


def backward_layer(upstream, pieces, hid_cos, hid_sin, seq_cos, seq_sin, weights):
    w_first, b_first, w_second, b_second, gain_first, shift_first, gain_second, shift_second = (
        weights
    )
    summed, normed, pre_act, hidden, second_sum = pieces
    _, second_back = jax.vjp(layer_norm, second_sum, gain_second, shift_second)
    d_second, d_gain_second, d_shift_second = second_back(upstream)
    branch_grad = d_second.astype(jnp.bfloat16)
    grad_w_second = contract_rows(hidden, branch_grad)
    grad_b_second = jnp.sum(branch_grad.astype(jnp.float32), axis=0)
    hidden_grad = contract_cols(branch_grad, w_second)
    _, gelu_back = jax.vjp(partial(jax.nn.gelu, approximate=True), pre_act)
    (act_full,) = gelu_back(hidden_grad)
    act_grad = act_full.astype(jnp.bfloat16)
    grad_w_first = contract_rows(normed.astype(jnp.bfloat16), act_grad)
    grad_b_first = jnp.sum(act_grad.astype(jnp.float32), axis=0)
    normed_grad = d_second + contract_cols(act_grad, w_first)
    _, first_back = jax.vjp(layer_norm, summed, gain_first, shift_first)
    d_summed, d_gain_first, d_shift_first = first_back(normed_grad)
    mix_grad = d_summed.astype(jnp.bfloat16)
    real_grad = jnp.dot(seq_cos, mix_grad, preferred_element_type=jnp.float32).astype(jnp.bfloat16)
    imag_grad = (-jnp.dot(seq_sin, mix_grad, preferred_element_type=jnp.float32)).astype(
        jnp.bfloat16
    )
    input_grad = (
        d_summed
        + jnp.dot(real_grad, hid_cos, preferred_element_type=jnp.float32)
        + jnp.dot(imag_grad, hid_sin, preferred_element_type=jnp.float32)
    )
    return (
        input_grad,
        (
            grad_w_first,
            grad_b_first,
            grad_w_second,
            grad_b_second,
            d_gain_first,
            d_shift_first,
            d_gain_second,
            d_shift_second,
        ),
    )


def select_slot(saved_items, first_slot, second_slot, is_first):
    blank_item = jax.tree.map(jnp.zeros_like, saved_items[0])
    first_item = saved_items[first_slot] if 0 <= first_slot < len(saved_items) else blank_item
    second_item = saved_items[second_slot]
    return jax.tree.map(partial(jnp.where, is_first), first_item, second_item)


def body(boundary, bucket_ids, w_in, b_in, w_out, b_out, gain_one, shift_one, gain_two, shift_two):
    section_index = lax.axis_index("section")
    layer_index = section_index % 2
    copy_index = section_index // 2
    is_first = layer_index == 0
    layer_float = layer_index.astype(jnp.float32)
    micro_count = bucket_ids.shape[1]
    feat_width = boundary.shape[2]
    slab_len = boundary.shape[1] // micro_count
    base_len = slab_len // 4
    slabs = boundary[0].reshape(micro_count, slab_len, feat_width)
    buckets = lax.dynamic_index_in_dim(bucket_ids, copy_index, 0, keepdims=False)
    w_in_piece = lax.dynamic_index_in_dim(w_in, layer_index, 0, keepdims=False)
    w_out_piece = lax.dynamic_index_in_dim(w_out, layer_index, 0, keepdims=False)
    w_first, w_second = (
        lax.all_gather(w_in_piece, "dp", axis=0, tiled=True),
        lax.all_gather(w_out_piece, "dp", axis=0, tiled=True),
    )
    small_params = tuple(
        (
            lax.dynamic_index_in_dim(param_array, layer_index, 0, keepdims=False)
            for param_array in (b_in, b_out, gain_one, shift_one, gain_two, shift_two)
        )
    )
    weights = (
        w_first,
        small_params[0],
        w_second,
        small_params[1],
        small_params[2],
        small_params[3],
        small_params[4],
        small_params[5],
    )
    hid_cos, hid_sin = hidden_tables(feat_width)

    def tables_for(micro_slot):
        slot_index = jnp.clip(micro_slot, 0, micro_count - 1)
        bucket_row = lax.dynamic_index_in_dim(buckets, slot_index, 0, keepdims=False)
        return block_tables(bucket_row, slab_len, base_len)

    received = jnp.zeros((slab_len, feat_width), jnp.bfloat16)
    grad_totals = tuple((jnp.zeros(param_array.shape, jnp.float32) for param_array in weights))
    shard_totals = None
    saved_inputs = []
    forward_rows = []
    input_grads = []
    for tick_num in range(micro_count + 2):
        own_rows = slabs[tick_num] if tick_num < micro_count else jnp.zeros_like(slabs[0])
        layer_input = jnp.where(is_first, own_rows, received)
        seq_cos, seq_sin = tables_for(tick_num - layer_index)
        out_rows, pieces = forward_layer(layer_input, hid_cos, hid_sin, seq_cos, seq_sin, weights)
        saved_inputs.append(layer_input)
        forward_rows.append(out_rows)
        back_slot = tick_num - 1
        own_cot = (
            slabs[back_slot].astype(jnp.float32)
            if 0 <= back_slot < micro_count
            else jnp.zeros((slab_len, feat_width), jnp.float32)
        )
        upstream = jnp.where(is_first, received.astype(jnp.float32), own_cot)
        back_cos, back_sin = tables_for(tick_num - 2 + layer_index)
        back_input = select_slot(saved_inputs, tick_num - 2, tick_num, is_first)
        _, back_pieces = forward_layer(back_input, hid_cos, hid_sin, back_cos, back_sin, weights)
        input_grad, tick_grads = backward_layer(
            upstream, back_pieces, hid_cos, hid_sin, back_cos, back_sin, weights
        )
        valid_mask = jnp.where(
            is_first, tick_num >= 2, (tick_num >= 1) & (tick_num <= micro_count)
        ).astype(jnp.float32)
        tick_grads = tuple((grad_piece * valid_mask for grad_piece in tick_grads))
        grad_totals = jax.tree.map(jnp.add, grad_totals, tick_grads)
        input_grads.append(input_grad)
        if tick_num <= micro_count:
            outgoing = jnp.where(
                is_first, out_rows.astype(jnp.bfloat16), input_grad.astype(jnp.bfloat16)
            )
            received = partner(outgoing, "section", 0)
    shard_totals = (
        lax.psum_scatter(grad_totals[0], "dp", scatter_dimension=0, tiled=True),
        lax.psum_scatter(grad_totals[1], "dp", scatter_dimension=0, tiled=True),
        lax.psum_scatter(grad_totals[2], "dp", scatter_dimension=0, tiled=True),
        lax.psum_scatter(grad_totals[3], "dp", scatter_dimension=0, tiled=True),
        lax.psum_scatter(grad_totals[4], "dp", scatter_dimension=0, tiled=True),
        lax.psum_scatter(grad_totals[5], "dp", scatter_dimension=0, tiled=True),
        lax.psum_scatter(grad_totals[6], "dp", scatter_dimension=0, tiled=True),
        lax.psum_scatter(grad_totals[7], "dp", scatter_dimension=0, tiled=True),
    )
    placed = tuple(
        (
            jnp.stack([piece_sum * (1.0 - layer_float), piece_sum * layer_float])
            for piece_sum in shard_totals
        )
    )
    layer_grads = (
        lax.psum(placed[0].astype(jnp.bfloat16), "section").astype(jnp.float32),
        lax.psum(placed[1].astype(jnp.bfloat16), "section").astype(jnp.float32),
        lax.psum(placed[2].astype(jnp.bfloat16), "section").astype(jnp.float32),
        lax.psum(placed[3].astype(jnp.bfloat16), "section").astype(jnp.float32),
        lax.psum(placed[4].astype(jnp.bfloat16), "section").astype(jnp.float32),
        lax.psum(placed[5].astype(jnp.bfloat16), "section").astype(jnp.float32),
        lax.psum(placed[6].astype(jnp.bfloat16), "section").astype(jnp.float32),
        lax.psum(placed[7].astype(jnp.bfloat16), "section").astype(jnp.float32),
    )
    result_rows = [
        jnp.where(is_first, input_grads[slot_num + 2], forward_rows[slot_num + 1])
        for slot_num in range(micro_count)
    ]
    result = jnp.stack(result_rows).reshape(1, micro_count * slab_len, feat_width)
    return (
        result,
        layer_grads[0],
        layer_grads[1],
        layer_grads[2],
        layer_grads[3],
        layer_grads[4],
        layer_grads[5],
        layer_grads[6],
        layer_grads[7],
    )


def solution(mesh):
    return jax.shard_map(
        body,
        mesh=mesh,
        in_specs=(
            P("section", "dp", None),
            P(None, "dp", None),
            P(None, "dp", None),
            P(),
            P(None, "dp", None),
            P(),
            P(),
            P(),
            P(),
            P(),
        ),
        out_specs=(
            P("section", "dp", None),
            P(None, "dp", None),
            P(None, "dp"),
            P(None, "dp", None),
            P(None, "dp"),
            P(None, "dp"),
            P(None, "dp"),
            P(None, "dp"),
            P(None, "dp"),
        ),
        check_vma=False,
    )
```

profile of v0, /device:TPU:0, one launch (start us, length us, event | category | flops | bytes accessed | tf_op | source)
XLA Modules:
  0.0 1015.3 jit_solution(7517837776995003062)
XLA Ops:
  21.6 24.7 %fusion.702 = bf16[512,512]{1,0:T(8,128)(2,1)S(1)} fusion(f32[512]{0:T(512)S(1)} %convert_rsqrt_fusion.5, s32[512]{0:T(512)S(1)} %convert_reduce_fusion.13, f32[512]{0:T(512)S(1)} %convert_element_type.578, pred[512]{0:T(512)(128)(4,1)S(1)} %get-tuple-element.97, s32[512]{0:T(512)S(1)} %bitcast.339, s32[512]{0:T(512)S(1)} %iota_subtract_fusion.5), kind=kLoop, calls=%fused_computation.290.clone.1.clone.2 | loop fusion | flops 3932160 | bytes 535040 | tf_op jit(solution)/shard_map/dot_general | solution.py:83
  46.3 10.9 %fusion.144 = f32[512,768]{1,0:T(8,128)} fusion(pred[]{:T(512)S(6)} %eq.591, bf16[1,1024,768]{2,1,0:T(8,128)(2,1)S(1)} %copy-done.2, bf16[512,512]{1,0:T(8,128)(2,1)S(1)} %fusion.702), kind=kOutput, calls=%fused_computation.263 | convolution fusion | flops 1014300672 | bytes 2884608 | tf_op jit(solution)/shard_map/dot_general | solution.py:83
  58.6 17.2 %fusion.603 = (f32[512]{0:T(512)S(1)}, f32[512,768]{1,0:T(8,128)}) fusion(f32[512,768]{1,0:T(8,128)} %fusion.144, pred[]{:T(512)S(6)} %eq.591, bf16[1,1024,768]{2,1,0:T(8,128)(2,1)S(1)} %copy-done.2, f32[512]{0:T(512)S(1)} %convert_rsqrt_fusion.5, s32[512]{0:T(512)S(1)} %convert_reduce_fusion.13, f32[512]{0:T(512)S(1)} %convert_element_type.578, ...), kind=kOutput, calls=%fused_computation.772 | convolution fusion | flops 408944128 | bytes 4736512 | tf_op jit(solution)/shard_map/dot_general | solution.py:83
  80.2 14.6 %fusion.700 = bf16[512,512]{1,0:T(8,128)(2,1)S(1)} fusion(f32[512]{0:T(512)S(1)} %convert_rsqrt_fusion.6, s32[512]{0:T(512)S(1)} %convert_reduce_fusion.14, f32[512]{0:T(512)S(1)} %convert_element_type.564, pred[512]{0:T(512)(128)(4,1)S(1)} %get-tuple-element.93, s32[512]{0:T(512)S(1)} %bitcast.343, s32[512]{0:T(512)S(1)} %iota_subtract_fusion.6), kind=kLoop, calls=%fused_computation.288.clone.clone.2 | loop fusion | flops 3932160 | bytes 535040 | tf_op jit(solution)/shard_map/dot_general | solution.py:83
  116.5 17.7 %fusion.605 = (f32[512]{0:T(512)S(1)}, f32[512,768]{1,0:T(8,128)S(1)}) fusion(f32[512,768]{1,0:T(8,128)} %fusion.143, pred[]{:T(512)S(6)} %eq.591, bf16[1,1024,768]{2,1,0:T(8,128)(2,1)S(1)} %copy-done.2, f32[512]{0:T(512)S(1)} %convert_rsqrt_fusion.6, s32[512]{0:T(512)S(1)} %convert_reduce_fusion.14, f32[512]{0:T(512)S(1)} %convert_element_type.564, ...), kind=kOutput, calls=%fused_computation.774 | convolution fusion | flops 408550912 | bytes 4735489 | tf_op jit(solution)/shard_map/dot_general | solution.py:83
  174.0 14.8 %negate_convert_fusion.3.clone.5 = bf16[512,768]{1,0:T(8,128)(2,1)S(1)} fusion(f32[512,768]{1,0:T(8,128)S(1)} %get-tuple-element.96, f32[512]{0:T(512)S(1)} %negate_multiply_fusion.6, f32[512]{0:T(512)S(1)} %convert_rsqrt_fusion.5, s32[512]{0:T(512)S(1)} %convert_reduce_fusion.13, f32[512]{0:T(512)S(1)} %convert_element_type.578, ...), kind=kOutput, calls=%fused_computation.200.clone.clone.clone.2 | convolution fusion | flops 408158208 | bytes 2372096 | tf_op jit(solution)/shard_map/dot_general | solution.py:118
  188.9 14.6 %convolution_convert_fusion.17.clone.5 = bf16[512,768]{1,0:T(8,128)(2,1)S(1)} fusion(f32[512,768]{1,0:T(8,128)S(1)} %get-tuple-element.96, f32[512]{0:T(512)S(1)} %negate_multiply_fusion.6, f32[512]{0:T(512)S(1)} %convert_rsqrt_fusion.5, s32[512]{0:T(512)S(1)} %convert_reduce_fusion.13, f32[512]{0:T(512)S(1)} %convert_element_type.578, ...), kind=kOutput, calls=%fused_computation.243.clone.clone.clone.2 | convolution fusion | flops 407764992 | bytes 2372096 | tf_op jit(solution)/shard_map/dot_general | solution.py:117
  211.3 11.1 %fusion.139 = f32[512,768]{1,0:T(8,128)S(1)} fusion(bf16[512,768]{1,0:T(8,128)(2,1)S(1)} %convolution_convert_fusion.17.clone.5), kind=kOutput, calls=%fused_computation.258 | convolution fusion | flops 610467840 | bytes 2359296 | tf_op jit(solution)/shard_map/dot_general | solution.py:123
  241.5 11.2 %collective-permute-done = bf16[512,768]{1,0:T(8,128)(2,1)S(1)} collective-permute-done((bf16[512,768]{1,0:T(8,128)(2,1)S(1)}, bf16[512,768]{1,0:T(8,128)(2,1)S(1)}, u32[]{:S(2)}, u32[]{:S(2)}) %collective-permute-start) | collective-permute-done | bytes 786464 | tf_op jit(solution)/shard_map/ppermute | solution.py:13
  283.3 11.2 %convolution_convert_fusion.8.clone.1.clone.5 = bf16[512,768]{1,0:T(8,128)(2,1)S(1)} fusion(bf16[512,768]{1,0:T(8,128)(2,1)S(1)} %bitcast_select_fusion.2), kind=kOutput, calls=%fused_computation.234.clone.clone.clone.clone.clone.2 | convolution fusion | flops 610861056 | bytes 1572864 | tf_op jit(solution)/shard_map/dot_general | solution.py:80
  294.5 14.5 %fusion.146 = f32[512,768]{1,0:T(8,128)S(1)} fusion(f32[512]{0:T(512)S(1)} %convert_rsqrt_fusion.3, s32[512]{0:T(512)S(1)} %convert_reduce_fusion.11, f32[512]{0:T(512)S(1)} %convert_element_type.608, pred[512]{0:T(512)(128)(4,1)S(1)} %get-tuple-element.91, s32[512]{0:T(512)S(1)} %bitcast.371, s32[512]{0:T(512)S(1)} %iota_subtract_fusion.3, ...), kind=kOutput, calls=%fused_computation.265 | convolution fusion | flops 406585344 | bytes 2370048 | tf_op jit(solution)/shard_map/dot_general | solution.py:83
  309.0 15.0 %fusion.609 = (f32[512]{0:T(512)S(1)}, f32[512,768]{1,0:T(8,128)S(1)}) fusion(f32[512,768]{1,0:T(8,128)S(1)} %fusion.146, bf16[512,768]{1,0:T(8,128)(2,1)S(1)} %bitcast_select_fusion.2, pred[]{:T(512)S(6)} %eq.591, f32[512]{0:T(512)S(1)} %convert_rsqrt_fusion.3, s32[512]{0:T(512)S(1)} %convert_reduce_fusion.11, f32[512]{0:T(512)S(1)} %convert_element_type.608, ...), kind=kOutput, calls=%fused_computation.776 | convolution fusion | flops 408550912 | bytes 4731393 | tf_op jit(solution)/shard_map/dot_general | solution.py:83
  346.2 14.9 %negate_convert_fusion.2.clone.5 = bf16[512,768]{1,0:T(8,128)(2,1)S(1)} fusion(f32[512,768]{1,0:T(8,128)S(1)} %get-tuple-element.88, f32[512]{0:T(512)S(1)} %negate_multiply_fusion.4, f32[512]{0:T(512)S(1)} %convert_rsqrt_fusion.3, s32[512]{0:T(512)S(1)} %convert_reduce_fusion.11, f32[512]{0:T(512)S(1)} %convert_element_type.608, ...), kind=kOutput, calls=%fused_computation.185.clone.clone.clone.2 | convolution fusion | flops 408158208 | bytes 2372096 | tf_op jit(solution)/shard_map/dot_general | solution.py:118
  361.0 14.6 %convolution_convert_fusion.16.clone.2 = bf16[512,768]{1,0:T(8,128)(2,1)S(1)} fusion(f32[512,768]{1,0:T(8,128)S(1)} %get-tuple-element.88, f32[512]{0:T(512)S(1)} %negate_multiply_fusion.4, f32[512]{0:T(512)S(1)} %convert_rsqrt_fusion.3, s32[512]{0:T(512)S(1)} %convert_reduce_fusion.11, f32[512]{0:T(512)S(1)} %convert_element_type.608, ...), kind=kOutput, calls=%fused_computation.242.clone.clone.clone | convolution fusion | flops 407764992 | bytes 2372096 | tf_op jit(solution)/shard_map/dot_general | solution.py:117
  375.6 14.5 %fusion.145 = f32[512,768]{1,0:T(8,128)S(1)} fusion(f32[512]{0:T(512)S(1)} %convert_rsqrt_fusion.4, s32[512]{0:T(512)S(1)} %convert_reduce_fusion.12, s32[512]{0:T(512)S(1)} %bitcast.369, f32[512]{0:T(512)S(1)} %convert_element_type.594, s32[512]{0:T(512)S(1)} %iota_subtract_fusion.4, pred[512]{0:T(512)(128)(4,1)S(1)} %get-tuple-element.85, ...), kind=kOutput, calls=%fused_computation.264 | convolution fusion | flops 406585344 | bytes 2370048 | tf_op jit(solution)/shard_map/dot_general | solution.py:83
  390.2 15.1 %fusion.611 = (f32[512]{0:T(512)S(1)}, f32[512,768]{1,0:T(8,128)S(1)}) fusion(f32[512,768]{1,0:T(8,128)S(1)} %fusion.145, bf16[512,768]{1,0:T(8,128)(2,1)S(1)} %bitcast_select_fusion.2, f32[512]{0:T(512)S(1)} %convert_rsqrt_fusion.4, s32[512]{0:T(512)S(1)} %convert_reduce_fusion.12, f32[512]{0:T(512)S(1)} %convert_element_type.594, ...), kind=kOutput, calls=%fused_computation.778 | convolution fusion | flops 408157696 | bytes 4731392 | tf_op jit(solution)/shard_map/dot_general | solution.py:83
  462.4 14.7 %fusion.147 = f32[512,768]{1,0:T(8,128)S(1)} fusion(f32[512]{0:T(512)S(1)} %copy-done.54, s32[512]{0:T(512)S(1)} %copy-done.40, f32[512]{0:T(512)S(1)} %copy-done.52, pred[512]{0:T(512)(128)(4,1)S(1)} %copy-done.66, s32[512]{0:T(512)S(1)} %bitcast.365, s32[512]{0:T(512)S(1)} %copy-done.58, bf16[512,768]{1,0:T(8,128)(2,1)S(1)} %convolution_convert_fusion.5.clone.5), kind=kOutput, calls=%fused_computation.266 | convolution fusion | flops 406585344 | bytes 2370048 | tf_op jit(solution)/shard_map/dot_general | solution.py:83
  486.6 15.3 %fusion.614 = (f32[512]{0:T(512)S(1)}, f32[512,768]{1,0:T(8,128)S(1)}) fusion(f32[512,768]{1,0:T(8,128)S(1)} %fusion.147, pred[]{:T(512)S(6)} %eq.591, bf16[512,768]{1,0:T(8,128)(2,1)S(1)} %collective-permute-done.1, bf16[1,1024,768]{2,1,0:T(8,128)(2,1)S(1)} %copy-done.2, f32[512]{0:T(512)S(1)} %copy-done.54, s32[512]{0:T(512)S(1)} %copy-done.40, ...), kind=kOutput, calls=%fused_computation.781 | convolution fusion | flops 409337344 | bytes 5522944 | tf_op jit(solution)/shard_map/dot_general | solution.py:83
  523.0 14.9 %negate_convert_fusion.1.clone.1.clone.5 = bf16[512,768]{1,0:T(8,128)(2,1)S(1)} fusion(f32[512,768]{1,0:T(8,128)S(1)} %get-tuple-element.78, f32[512]{0:T(512)S(1)} %negate_multiply_fusion.2, f32[512]{0:T(512)S(1)} %copy-done.54, s32[512]{0:T(512)S(1)} %copy-done.40, f32[512]{0:T(512)S(1)} %copy-done.52, ...), kind=kOutput, calls=%fused_computation.174.clone.clone.clone.clone.clone.2 | convolution fusion | flops 408158208 | bytes 2372096 | tf_op jit(solution)/shard_map/dot_general | solution.py:118
  537.9 14.6 %convolution_convert_fusion.15.clone.2 = bf16[512,768]{1,0:T(8,128)(2,1)S(1)} fusion(f32[512,768]{1,0:T(8,128)S(1)} %get-tuple-element.78, f32[512]{0:T(512)S(1)} %negate_multiply_fusion.2, f32[512]{0:T(512)S(1)} %copy-done.54, s32[512]{0:T(512)S(1)} %copy-done.40, f32[512]{0:T(512)S(1)} %copy-done.52, pred[512]{0:T(512)(128)(4,1)S(1)} %copy-done.66, ...), kind=kOutput, calls=%fused_computation.241.clone.clone.clone | convolution fusion | flops 407764992 | bytes 2372096 | tf_op jit(solution)/shard_map/dot_general | solution.py:117
  573.8 14.5 %fusion.148 = f32[512,768]{1,0:T(8,128)S(1)} fusion(f32[512]{0:T(512)S(1)} %copy-done.53, s32[512]{0:T(512)S(1)} %copy-done.38, s32[512]{0:T(512)S(1)} %bitcast.363, f32[512]{0:T(512)S(1)} %copy-done.51, s32[512]{0:T(512)S(1)} %copy-done.56, pred[512]{0:T(512)(128)(4,1)S(1)} %copy-done.65, bf16[512,768]{1,0:T(8,128)(2,1)S(1)} %convolution_convert_fusion.3.clone.5), kind=kOutput, calls=%fused_computation.267 | convolution fusion | flops 406585344 | bytes 2370048 | tf_op jit(solution)/shard_map/dot_general | solution.py:83
  598.7 14.9 %fusion.613 = (f32[512]{0:T(512)S(1)}, f32[512,768]{1,0:T(8,128)S(1)}) fusion(f32[512,768]{1,0:T(8,128)S(1)} %fusion.148, bf16[512,768]{1,0:T(8,128)(2,1)S(1)} %collective-permute-done.1, pred[]{:T(512)S(6)} %eq.591, f32[512]{0:T(512)S(1)} %copy-done.53, s32[512]{0:T(512)S(1)} %copy-done.38, f32[512]{0:T(512)S(1)} %copy-done.51, ...), kind=kOutput, calls=%fused_computation.780 | convolution fusion | flops 408550912 | bytes 4731393 | tf_op jit(solution)/shard_map/dot_general | solution.py:83
  660.0 14.5 %fusion.149 = f32[512,768]{1,0:T(8,128)S(1)} fusion(f32[512]{0:T(512)S(1)} %copy-done.48, s32[512]{0:T(512)S(1)} %copy-done.36, f32[512]{0:T(512)S(1)} %copy-done.47, pred[512]{0:T(512)(128)(4,1)S(1)} %copy-done.64, s32[512]{0:T(512)S(1)} %bitcast.359, s32[512]{0:T(512)S(1)} %copy-done.50, bf16[512,768]{1,0:T(8,128)(2,1)S(1)} %convolution_convert_fusion.1.clone.5), kind=kOutput, calls=%fused_computation.268 | convolution fusion | flops 406585344 | bytes 2370048 | tf_op jit(solution)/shard_map/dot_general | solution.py:83
  684.9 14.8 %fusion.619 = (f32[512]{0:T(512)S(1)}, f32[512,768]{1,0:T(8,128)S(1)}) fusion(f32[512,768]{1,0:T(8,128)S(1)} %fusion.149, bf16[512,768]{1,0:T(8,128)(2,1)S(1)} %bitcast_select_fusion.2, bf16[512,768]{1,0:T(8,128)(2,1)S(1)} %collective-permute-done.2, pred[]{:T(512)S(6)} %eq.591, f32[512]{0:T(512)S(1)} %copy-done.48, s32[512]{0:T(512)S(1)} %copy-done.36, ...), kind=kOutput, calls=%fused_computation.784 | convolution fusion | flops 408944128 | bytes 5517825 | tf_op jit(solution)/shard_map/dot_general | solution.py:83
  711.5 15.6 %multiply_add_fusion = f32[3072,768]{1,0:T(8,128)} fusion(f32[3072,768]{1,0:T(8,128)} %fusion.595, f32[3072,768]{1,0:T(8,128)} %fusion.594, f32[3072,768]{1,0:T(8,128)} %fusion.593, bf16[512,768]{1,0:T(8,128)(2,1)S(1)} %get-tuple-element.70, f32[]{:T(128)S(6)} %convert_element_type.667, f32[]{:T(128)S(6)} %convert_element_type.666, ...), kind=kOutput, calls=%fused_computation.3 | convolution fusion | flops 2445803520 | bytes 44838920 | tf_op jit(solution)/shard_map/dot_general | solution.py:62
  757.1 15.6 %multiply_add_fusion.1 = f32[768,3072]{1,0:T(8,128)} fusion(f32[768,3072]{1,0:T(8,128)} %fusion.583, f32[768,3072]{1,0:T(8,128)} %fusion.586, f32[768,3072]{1,0:T(8,128)} %fusion.589, bf16[512,3072]{1,0:T(8,128)(2,1)S(1)} %get-tuple-element.160, f32[]{:T(128)S(6)} %convert_element_type.667, f32[]{:T(128)S(6)} %convert_element_type.666, ...), kind=kOutput, calls=%fused_computation.4 | convolution fusion | flops 2432040960 | bytes 42477576 | tf_op jit(solution)/shard_map/dot_general | solution.py:62
  783.5 28.1 %all-reduce.6 = (f32[3072]{0:T(1024)S(1)}, f32[768]{0:T(1024)S(1)}, f32[768]{0:T(1024)S(1)}, f32[768]{0:T(1024)S(1)}, f32[768]{0:T(1024)S(1)}, /*index=5*/f32[768]{0:T(1024)S(1)}) all-reduce(f32[3072]{0:T(1024)S(1)} %multiply_add_fusion.11, f32[768]{0:T(1024)S(1)} %multiply_add_fusion.16, ...), channel_id=5, replica_groups=mesh['section'=4,'dp'=8] {'dp'}, use_global_device_ids=true, to_apply=%region_78.80.clone | all-reduce | flops 6912 | bytes 55296
  830.6 97.5 %reduce-scatter.3.cloned.1.call-done = f32[96,3072]{1,0:T(8,128)} async-done(((f32[768,3072]{1,0:T(8,128)}), f32[96,3072]{1,0:T(8,128)}) %reduce-scatter.3.cloned.1.call-update) | async-done | bytes 1179664 | tf_op jit(solution)/shard_map/reduce_scatter | solution.py:227
  932.7 14.6 %convolution_convert_fusion.14.clone.2 = bf16[512,768]{1,0:T(8,128)(2,1)S(1)} fusion(f32[512,768]{1,0:T(8,128)S(1)} %get-tuple-element.72, f32[512]{0:T(512)S(1)} %negate_multiply_fusion, f32[512]{0:T(512)S(1)} %copy-done.48, s32[512]{0:T(512)S(1)} %copy-done.36, f32[512]{0:T(512)S(1)} %copy-done.47, pred[512]{0:T(512)(128)(4,1)S(1)} %copy-done.64, ...), kind=kOutput, calls=%fused_computation.240.clone.clone.clone | convolution fusion | flops 407764992 | bytes 2372096 | tf_op jit(solution)/shard_map/dot_general | solution.py:117
  947.3 11.1 %fusion.142 = f32[512,768]{1,0:T(8,128)S(1)} fusion(bf16[512,768]{1,0:T(8,128)(2,1)S(1)} %convolution_convert_fusion.14.clone.2), kind=kOutput, calls=%fused_computation.261 | convolution fusion | flops 610467840 | bytes 2359296 | tf_op jit(solution)/shard_map/dot_general | solution.py:123
  958.4 14.6 %negate_convert_fusion.clone.5 = bf16[512,768]{1,0:T(8,128)(2,1)S(1)} fusion(f32[512,768]{1,0:T(8,128)S(1)} %get-tuple-element.72, f32[512]{0:T(512)S(1)} %negate_multiply_fusion, f32[512]{0:T(512)S(1)} %copy-done.48, s32[512]{0:T(512)S(1)} %copy-done.36, f32[512]{0:T(512)S(1)} %copy-done.47, pred[512]{0:T(512)(128)(4,1)S(1)} %copy-done.64, ...), kind=kOutput, calls=%fused_computation.156.clone.clone.clone.2 | convolution fusion | flops 408158208 | bytes 2372096 | tf_op jit(solution)/shard_map/dot_general | solution.py:118
  984.7 19.2 %all-reduce.11.cloned.1.call-done = (bf16[2,96,3072]{2,1,0:T(8,128)(2,1)}, bf16[2,384,768]{2,1,0:T(8,128)(2,1)}) async-done(((bf16[2,96,3072]{2,1,0:T(8,128)(2,1)}, bf16[2,384,768]{2,1,0:T(8,128)(2,1)}), (bf16[2,96,3072]{2,1,0:T(8,128)(2,1)}, bf16[2,384,768]{2,1,0:T(8,128)(2,1)})) %all-reduce.11.cloned.1.call-update) | async-done | bytes 2359312 | tf_op jit(solution)/shard_map/psum | solution.py:243
  (404 shorter events, 427.1 us)
Async XLA Ops:
  7.2 135.2 %all-gather.5.cloned.1.call-start = ((), (), s32[]{:S(2)}) async-start(), calls=%async_computation.4 | async-start | bytes 5308416 | tf_op jit(solution)/shard_map/all_gather | solution.py:163
  9.3 141.3 %all-gather.7.cloned.1.call-start = ((), (), s32[]{:S(2)}) async-start(), calls=%async_computation.5 | async-start | bytes 5308416 | tf_op jit(solution)/shard_map/all_gather | solution.py:164
  11.3 816.7 %reduce-scatter.5.cloned.1.call-start = ((), (), s32[]{:S(2)}) async-start(), calls=%async_computation.3 | async-start | bytes 10616832 | tf_op jit(solution)/shard_map/reduce_scatter | solution.py:229
  58.6 19.7 %copy-start.59 = (f32[2,768]{1,0:T(2,128)S(1)}, f32[2,768]{1,0:T(2,128)}, u32[]{:S(2)}) copy-start(f32[2,768]{1,0:T(2,128)} %param.21) | copy-start | bytes 18436
  58.6 19.7 %copy-start.60 = (f32[2,768]{1,0:T(2,128)S(1)}, f32[2,768]{1,0:T(2,128)}, u32[]{:S(2)}) copy-start(f32[2,768]{1,0:T(2,128)} %param.18) | copy-start | bytes 18436
  58.6 19.7 %copy-start.61 = (f32[2,768]{1,0:T(2,128)S(1)}, f32[2,768]{1,0:T(2,128)}, u32[]{:S(2)}) copy-start(f32[2,768]{1,0:T(2,128)} %param.19) | copy-start | bytes 18436
  58.6 19.8 %copy-start.62 = (f32[2,768]{1,0:T(2,128)S(1)}, f32[2,768]{1,0:T(2,128)}, u32[]{:S(2)}) copy-start(f32[2,768]{1,0:T(2,128)} %param.17) | copy-start | bytes 18436
  58.6 19.8 %copy-start.63 = (f32[2,768]{1,0:T(2,128)S(1)}, f32[2,768]{1,0:T(2,128)}, u32[]{:S(2)}) copy-start(f32[2,768]{1,0:T(2,128)} %param.20) | copy-start | bytes 18436
  78.4 95.0 %copy-start.17 = (f32[512]{0:T(512)}, f32[512]{0:T(512)S(1)}, u32[]{:S(2)}) copy-start(f32[512]{0:T(512)S(1)} %broadcast_multiply_fusion.12) | copy-start | bytes 6148
  116.5 25.9 %copy-start.42 = (f32[2,3072]{1,0:T(2,128)S(1)}, f32[2,3072]{1,0:T(2,128)}, u32[]{:S(2)}) copy-start(f32[2,3072]{1,0:T(2,128)} %param.15) | copy-start | bytes 73732
  137.4 36.0 %copy-start.31 = (f32[512]{0:T(512)}, f32[512]{0:T(512)S(1)}, u32[]{:S(2)}) copy-start(f32[512]{0:T(512)S(1)} %fusion.371) | copy-start | bytes 6148
  232.1 20.6 %collective-permute-start = (bf16[512,768]{1,0:T(8,128)(2,1)S(1)}, bf16[512,768]{1,0:T(8,128)(2,1)S(1)}, u32[]{:S(2)}, u32[]{:S(2)}) collective-permute-start(bf16[512,768]{1,0:T(8,128)(2,1)S(1)} %fusion.156), channel_id=1, source_target_pairs={{0,8},{8,0},{16,24},{24,16},{1,9},{9,1},{17,25},{25,17},{2,10},{10... | collective-permute-start | bytes 2359304 | tf_op jit(solution)/shard_map/ppermute | solution.py:13
  323.9 21.5 %copy-start.4 = (f32[512,768]{1,0:T(8,128)}, f32[512,768]{1,0:T(8,128)S(1)}, u32[]{:S(2)}) copy-start(f32[512,768]{1,0:T(8,128)S(1)} %get-tuple-element.135) | copy-start | bytes 4718596
  324.0 21.5 %copy-start.19 = (f32[512]{0:T(512)}, f32[512]{0:T(512)S(1)}, u32[]{:S(2)}) copy-start(f32[512]{0:T(512)S(1)} %broadcast_multiply_fusion.8) | copy-start | bytes 6148
  324.3 21.2 %copy-start.33 = (f32[512]{0:T(512)}, f32[512]{0:T(512)S(1)}, u32[]{:S(2)}) copy-start(f32[512]{0:T(512)S(1)} %fusion.373) | copy-start | bytes 6148
  434.0 18.9 %collective-permute-start.1 = (bf16[512,768]{1,0:T(8,128)(2,1)S(1)}, bf16[512,768]{1,0:T(8,128)(2,1)S(1)}, u32[]{:S(2)}, u32[]{:S(2)}) collective-permute-start(bf16[512,768]{1,0:T(8,128)(2,1)S(1)} %fusion.157), channel_id=1, source_target_pairs={{0,8},{8,0},{16,24},{24,16},{1,9},{9,1},{17,25},{25,17},{2,10},{10... | collective-permute-start | bytes 2359304 | tf_op jit(solution)/shard_map/ppermute | solution.py:13
  442.4 19.9 %copy-start.40 = (s32[512]{0:T(512)S(1)}, s32[512]{0:T(512)}, u32[]{:S(2)}) copy-start(s32[512]{0:T(512)} %copy-done.39) | copy-start | bytes 6148
  442.4 19.9 %copy-start.52 = (f32[512]{0:T(512)S(1)}, f32[512]{0:T(512)}, u32[]{:S(2)}) copy-start(f32[512]{0:T(512)} %convert_element_type.626) | copy-start | bytes 6148
  442.4 19.9 %copy-start.54 = (f32[512]{0:T(512)S(1)}, f32[512]{0:T(512)}, u32[]{:S(2)}) copy-start(f32[512]{0:T(512)} %convert_rsqrt_fusion.2) | copy-start | bytes 6148
  442.4 19.9 %copy-start.57 = (s32[512,1]{0,1:T(1,128)S(1)}, s32[512,1]{0,1:T(1,128)}, u32[]{:S(2)}) copy-start(s32[512,1]{0,1:T(1,128)} %get-tuple-element.82) | copy-start | bytes 6148
  442.4 19.9 %copy-start.58 = (s32[512]{0:T(512)S(1)}, s32[512]{0:T(512)}, u32[]{:S(2)}) copy-start(s32[512]{0:T(512)} %iota_subtract_fusion.2) | copy-start | bytes 6148
  442.4 19.9 %copy-start.66 = (pred[512]{0:T(512)(128)(4,1)S(1)}, pred[512]{0:T(512)(128)(4,1)}, u32[]{:S(2)}) copy-start(pred[512]{0:T(512)(128)(4,1)} %get-tuple-element.81) | copy-start | bytes 1540
  501.9 20.4 %copy-start.6 = (f32[512,768]{1,0:T(8,128)}, f32[512,768]{1,0:T(8,128)S(1)}, u32[]{:S(2)}) copy-start(f32[512,768]{1,0:T(8,128)S(1)} %get-tuple-element.146) | copy-start | bytes 4718596
  631.9 18.0 %collective-permute-start.2 = (bf16[512,768]{1,0:T(8,128)(2,1)S(1)}, bf16[512,768]{1,0:T(8,128)(2,1)S(1)}, u32[]{:S(2)}, u32[]{:S(2)}) collective-permute-start(bf16[512,768]{1,0:T(8,128)(2,1)S(1)} %get-tuple-element.152), channel_id=1, source_target_pairs={{0,8},{8,0},{16,24},{24,16},{1,9},{9,1},{17,25},{25,17},{2,10},{10... | collective-permute-start | bytes 2359304 | tf_op jit(solution)/shard_map/ppermute | solution.py:13
  639.7 20.3 %copy-start.36 = (s32[512]{0:T(512)S(1)}, s32[512]{0:T(512)}, u32[]{:S(2)}) copy-start(s32[512]{0:T(512)} %copy-done.35) | copy-start | bytes 6148
  639.7 20.3 %copy-start.47 = (f32[512]{0:T(512)S(1)}, f32[512]{0:T(512)}, u32[]{:S(2)}) copy-start(f32[512]{0:T(512)} %convert_element_type.654) | copy-start | bytes 6148
  639.7 20.3 %copy-start.48 = (f32[512]{0:T(512)S(1)}, f32[512]{0:T(512)}, u32[]{:S(2)}) copy-start(f32[512]{0:T(512)} %convert_rsqrt_fusion) | copy-start | bytes 6148
  639.7 20.3 %copy-start.49 = (s32[512,1]{0,1:T(1,128)S(1)}, s32[512,1]{0,1:T(1,128)}, u32[]{:S(2)}) copy-start(s32[512,1]{0,1:T(1,128)} %get-tuple-element.76) | copy-start | bytes 6148
  639.7 20.3 %copy-start.50 = (s32[512]{0:T(512)S(1)}, s32[512]{0:T(512)}, u32[]{:S(2)}) copy-start(s32[512]{0:T(512)} %iota_subtract_fusion) | copy-start | bytes 6148
  639.7 20.3 %copy-start.64 = (pred[512]{0:T(512)(128)(4,1)S(1)}, pred[512]{0:T(512)(128)(4,1)}, u32[]{:S(2)}) copy-start(pred[512]{0:T(512)(128)(4,1)} %get-tuple-element.75) | copy-start | bytes 1540
  727.2 200.9 %reduce-scatter.3.cloned.1.call-start = ((), (), s32[]{:S(2)}) async-start(), calls=%async_computation.2 | async-start | bytes 10616832 | tf_op jit(solution)/shard_map/reduce_scatter | solution.py:227
  772.7 231.2 %all-reduce.11.cloned.1.call-start = ((), (), s32[]{:S(2)}) async-start(), calls=%async_computation.6 | async-start | bytes 4718592 | tf_op jit(solution)/shard_map/psum | solution.py:243
  (59 other events, 433.1 us)
Sparse Core Ops, SparseCore 0:
  9.7 54.4 all-gather.4
  65.8 50.5 all-gather.6
  727.3 100.7 reduce-scatter.4
  830.2 97.8 reduce-scatter.2
  931.1 72.7 all-reduce.10
where the time goes:
time: 1020 us
  matrix products  706 us (69%)
  waiting for transfers between devices  151 us (15%)
  other arithmetic  87.2 us (9%)
  blocking collectives  38 us (4%)
  between operations  16.9 us (2%)
    dot_general x7, matrix products, forward_layer(): jnp.dot(seq_sin, imag_part, preferred_element_type=jnp.float32)  110 us
    reduce_scatter x1, waiting for transfers between devices, body(): lax.psum_scatter(grad_totals[0], 'dp', scatter_dimension=0, tiled=True)  97.5 us
    dot_general x7, matrix products, forward_layer(): jnp.dot(seq_cos, real_part, preferred_element_type=jnp.float32)  94.6 us
    dot_general x7, matrix products, forward_layer(): jnp.dot(layer_input, hid_sin, preferred_element_type=jnp.float32)  71.5 us
    dot_general x8, matrix products, contract_rows(): lax.dot_general(left, right, (((0,), (0,)), ((), ())), preferred_element_...  71.5 us
    dot_general x4, matrix products, backward_layer(): jnp.dot(seq_sin, mix_grad, preferred_element_type=jnp.float32)  59.2 us
    dot_general x4, matrix products, backward_layer(): jnp.dot(seq_cos, mix_grad, preferred_element_type=jnp.float32)  58.4 us
    dot_general x5, matrix products, forward_layer(): jnp.dot(layer_input, hid_cos, preferred_element_type=jnp.float32)  50.4 us
  transfers between devices with their start and end apart: 8, of which 6 were waited for; matrix products, arithmetic and copies ran while one was open for 27% of the time, Pallas kernels for 0%

commit v1 on v0

v1 whole, which is shorter than its diff:
```python
from functools import partial
import math

import jax
import jax.numpy as jnp
import numpy as np
from jax import lax
from jax.experimental import pallas as pl
from jax.experimental.pallas import tpu as pltpu
from jax.sharding import PartitionSpec as P

AXES = ("section", "dp")
F32 = jnp.float32
BF16 = jnp.bfloat16


class Place:
    def __init__(self):
        self.n_section = lax.axis_size("section")
        self.n_dp = lax.axis_size("dp")
        self.chips = self.n_dp // 2
        self.section = lax.axis_index("section")
        self.dp = lax.axis_index("dp")
        self.chip = self.dp // 2
        self.core = self.dp % 2

    def permute(self, value, target):
        pairs = []
        for section in range(self.n_section):
            for chip in range(self.chips):
                for core in range(2):
                    place = target(section, chip, core)
                    if place is not None:
                        to_section, to_chip, to_core = place
                        pairs.append(
                            (
                                section * self.n_dp + chip * 2 + core,
                                to_section * self.n_dp + to_chip * 2 + to_core,
                            )
                        )
        return lax.ppermute(value, AXES, pairs)

    def swap_core(self, value):
        return self.permute(value, lambda s, z, c: (s, z, 1 - c))

    def plane_one(self, value):
        return self.permute(value, lambda s, z, c: (s ^ (1 + c), z, c))

    def plane_two(self, value):
        return self.permute(value, lambda s, z, c: (s ^ (2 - c), z, c))

    def shift_chip(self, value, apart):
        return self.permute(value, lambda s, z, c: (s, (z + apart) % self.chips, c))


def dft_tables(length):
    positions = np.arange(length)
    angles = (positions[:, None] * positions[None, :] % length) * (2.0 * math.pi) / length
    scaling = 1.0 / math.sqrt(length)
    return (np.cos(angles) * scaling, np.sin(angles) * scaling)


def sequence_tiles(base_len):
    cos_tiles, sin_tiles = [], []
    for parts in (1, 2, 4):
        cos_table, sin_table = dft_tables(parts * base_len)
        for i in range(parts):
            for j in range(parts):
                window = (
                    slice(i * base_len, (i + 1) * base_len),
                    slice(j * base_len, (j + 1) * base_len),
                )
                cos_tiles.append(cos_table[window])
                sin_tiles.append(sin_table[window])
    cos_tiles.append(np.zeros((base_len, base_len)))
    sin_tiles.append(np.zeros((base_len, base_len)))
    return np.stack(cos_tiles).astype(BF16), np.stack(sin_tiles).astype(BF16)


def tile_numbers(bucket_row, slots):
    parts = jnp.where(bucket_row < 3, 1 << jnp.minimum(bucket_row, 2), 0)
    ends = jnp.cumsum(parts)
    where = jnp.arange(slots, dtype=jnp.int32)
    segment = jnp.sum((where[:, None] >= ends[None, :]).astype(jnp.int32), axis=1)
    one_hot = (segment[:, None] == jnp.arange(slots)[None, :]).astype(jnp.int32)
    start = jnp.sum(one_hot * (ends - parts)[None, :], axis=1)
    size = jnp.sum(one_hot * parts[None, :], axis=1)
    first = jnp.where(size == 1, 0, jnp.where(size == 2, 1, 5))
    place = where - start
    numbers = first[:, None] + place[:, None] * size[:, None] + place[None, :]
    return jnp.where(segment[:, None] == segment[None, :], numbers, 21)


class Spot:
    def __init__(self):
        self.section = lax.axis_index("section")
        dp = lax.axis_index("dp")
        self.chip, self.core = dp // 2, dp % 2


def plane_bits(core):
    return 1 + core, 2 - core


def rows_at(start, size):
    return pl.ds(pl.multiple_of(start, size), size)


class Loader:
    def __init__(self, layer, sources, scratch, sems, by_rows):
        self.sems = sems
        self.started = 0
        chunks, width = scratch.shape[0], scratch.shape[2]
        self.chunks = []
        if len(sources) == 1:
            for chunk in range(chunks):
                part = pl.ds(chunk * width, width)
                source = sources[0].at[part, :] if by_rows else sources[0].at[:, part]
                self.chunks.append((chunk, [self.start(source, scratch.at[chunk])]))
            return
        spot = Spot()
        chips = lax.axis_size("dp") // 2
        piece = sources[1].shape[1]
        if by_rows:
            for apart in range(chips):
                chip = (spot.chip + chips - apart) % chips
                copies = []
                for other in range(2):
                    own, near, far = sources[3 * other : 3 * other + 3]
                    core = (spot.core + other) % 2
                    bit_one, bit_two = plane_bits(core)
                    target = scratch.at[chip]
                    if apart == 0:
                        shard = rows_at(core * 4 * piece, 4 * piece)
                        copies.append(self.start(own.at[layer], target.at[shard, :]))
                        continue
                    for source, quarter in (
                        (near.at[apart - 1], spot.section),
                        (near.at[chips + apart - 2], spot.section ^ bit_one),
                        (far.at[apart - 1], spot.section ^ bit_two),
                        (far.at[chips + apart - 2], spot.section ^ 3),
                    ):
                        rows = rows_at((core * 4 + quarter) * piece, piece)
                        copies.append(self.start(source, target.at[rows, :]))
                self.chunks.append((chip, copies))
            return
        first, rest = [], []
        for other in range(2):
            own, near, far = sources[3 * other : 3 * other + 3]
            core = (spot.core + other) % 2
            bit_one, bit_two = plane_bits(core)
            for apart in range(chips):
                chip = (spot.chip + chips - apart) % chips
                rows = rows_at((2 * chip + core) * piece, piece)
                for turn, flip in enumerate((0, bit_one, bit_two, 3)):
                    quarter = spot.section ^ flip
                    if apart == 0:
                        columns = rows_at(quarter * width, width)
                        source = own.at[layer, :, columns]
                    else:
                        source = (near, far)[turn // 2].at[(turn % 2) * (chips - 1) + apart - 1]
                    copy = self.start(source, scratch.at[quarter, rows, :])
                    (rest if turn else first).append(copy)
        self.chunks.append((spot.section, first))
        self.chunks.append((spot.section ^ 1, rest))
        self.chunks.append((spot.section ^ 2, []))
        self.chunks.append((spot.section ^ 3, []))

    def start(self, source, target):
        copy = pltpu.make_async_copy(source, target, self.sems.at[self.started])
        copy.start()
        self.started += 1
        return copy

    def __iter__(self):
        for chunk, copies in self.chunks:
            for copy in copies:
                copy.wait()
            yield chunk


class Storer:
    def __init__(self, outs, tiles, sems, by_rows):
        self.outs, self.tiles, self.sems, self.by_rows = outs, tiles, sems, by_rows
        self.copies = []

    def start(self, source, target):
        copy = pltpu.make_async_copy(source, target, self.sems.at[len(self.copies)])
        copy.start()
        self.copies.append(copy)

    def store(self, chunk):
        tile = self.tiles.at[chunk]
        width = tile.shape[0]
        if len(self.outs) == 1:
            part = pl.ds(chunk * width, width)
            out = self.outs[0]
            self.start(tile, out.at[part, :] if self.by_rows else out.at[:, part])
            return
        spot = Spot()
        chips = lax.axis_size("dp") // 2
        piece = self.outs[0].shape[2]
        for other in range(2):
            out = self.outs[other]
            core = (spot.core + other) % 2
            bit_one, _ = plane_bits(core)

            def slot_of(quarter):
                flip = quarter ^ spot.section
                side = jnp.where(flip == bit_one, 0, 2)
                return jnp.where(flip == 3, 1, jnp.where(flip == 0, 3, side))

            for part in range(4 if self.by_rows else chips):
                if self.by_rows:
                    chip, quarter = chunk, part
                    rows = rows_at((core * 4 + quarter) * piece, piece)
                else:
                    chip, quarter = part, chunk
                    rows = rows_at((2 * chip + core) * piece, piece)
                apart = (chip + chips - spot.chip) % chips
                self.start(tile.at[rows, :], out.at[slot_of(quarter), apart])

    def finish(self):
        for copy in self.copies:
            copy.wait()


def gather_weight(place, shard, by_rows):
    if by_rows:
        piece_rows = shard.shape[0] // 4
        piece = lax.dynamic_slice_in_dim(shard, place.section * piece_rows, piece_rows, 0)
    else:
        width = shard.shape[1] // 4
        piece = lax.dynamic_slice_in_dim(shard, place.section * width, width, 1)
    along = jnp.stack([place.shift_chip(piece, apart) for apart in range(1, place.chips)])
    near = jnp.concatenate([along, place.plane_one(along)])
    far = place.plane_two(near)
    return near, far, place.swap_core(near), place.swap_core(far)


def scatter_grad(place, own, other):
    from_core = place.swap_core(other)
    wide = lambda value: value.astype(F32)
    first = (wide(own[0:2]) + wide(from_core[0:2])).astype(BF16)
    from_one = place.plane_one(first)
    second = (wide(own[2]) + wide(from_core[2]) + wide(from_one[1])).astype(BF16)
    from_two = place.plane_two(second)
    mine = wide(own[3]) + wide(from_core[3]) + wide(from_one[0]) + wide(from_two)
    total = mine[0]
    for apart in range(1, place.chips):
        total = total + wide(place.shift_chip(mine[apart].astype(BF16), apart))
    return total.astype(BF16)


def share_sections(place, piece, row_pieces):
    from_one = place.plane_one(piece)
    from_two = place.plane_two(jnp.stack([piece, from_one]))
    core_zero = place.core == 0
    quarters = [
        piece,
        jnp.where(core_zero, from_one, from_two[0]),
        jnp.where(core_zero, from_two[0], from_one),
        from_two[1],
    ]
    low_bit = place.section % 2 == 1
    high_bit = place.section // 2 == 1
    quarters = [jnp.where(low_bit, quarters[i ^ 1], quarters[i]) for i in range(4)]
    quarters = [jnp.where(high_bit, quarters[i ^ 2], quarters[i]) for i in range(4)]
    return jnp.concatenate(quarters, axis=0 if row_pieces else 1).astype(F32)


def sum_small(place, packed):
    total = packed + place.swap_core(packed)
    total = total + place.permute(total, lambda s, z, c: (s ^ 1, z, c))
    total = total + place.permute(total, lambda s, z, c: (s ^ 2, z, c))
    total = total + place.permute(total, lambda s, z, c: (s, z ^ 1, c))
    total = total + place.permute(total, lambda s, z, c: (s, z ^ 2, c))
    return lax.dynamic_index_in_dim(total, place.dp, 0, keepdims=False)


ROW_STEP = 256


def dot(left, right, dims=((1,), (0,))):
    return lax.dot_general(left, right, (dims, ((), ())), preferred_element_type=F32)


def norm(values):
    center = jnp.mean(values, axis=-1, keepdims=True)
    offsets = values - center
    inverse = lax.rsqrt(jnp.mean(offsets * offsets, axis=-1, keepdims=True) + 1e-05)
    return offsets * inverse, inverse


def norm_back(upstream, unit, inverse, gain):
    scaled = upstream * gain
    center = jnp.mean(scaled, axis=-1, keepdims=True)
    along = jnp.mean(scaled * unit, axis=-1, keepdims=True)
    return inverse * (scaled - center - unit * along)


def gelu_both(v):
    scale = math.sqrt(2.0 / math.pi)
    square = v * v
    half = 0.5 + 0.5 * jnp.tanh(v * (scale + (scale * 0.044715) * square))
    spread = (2.0 * half) * (1.0 - half)
    return v * half, half + (v * spread) * (scale + (3.0 * scale * 0.044715) * square)


def row_steps(count):
    step = min(ROW_STEP, count)

    def run(function):
        def one(i, carry):
            function(rows_at(i * step, step))
            return carry

        lax.fori_loop(0, count // step, one, 0)

    return run


def column_sum(values):
    return jnp.sum(values, axis=0, keepdims=True)


def mix_forward(rows, hid_cos, hid_sin, seq_cos, seq_sin, gain, shift, real, imag, outs):
    unit, inverse, normed_low, normed_turned = outs

    @row_steps(rows.shape[0])
    def _(at):
        real[at, :] = dot(rows[at, :], hid_cos[...]).astype(BF16)
        imag[at, :] = dot(rows[at, :], hid_sin[...]).astype(BF16)

    @row_steps(rows.shape[0])
    def _(at):
        mixed = dot(seq_cos[at, :], real[...]) - dot(seq_sin[at, :], imag[...])
        unit_rows, inverse_rows = norm(rows[at, :].astype(F32) + mixed)
        unit[at, :] = unit_rows
        inverse[at, :] = inverse_rows
        normed = (unit_rows * gain[...] + shift[...]).astype(BF16)
        normed_low[at, :] = normed
        normed_turned[:, at] = normed.T


def first_mix_kernel(numbers, rows, hid_cos, hid_sin, cos_tiles, sin_tiles, gain, shift, *refs):
    seq_cos, seq_sin = refs[0:2]
    outs, (real, imag) = refs[2:6], refs[6:]
    base = cos_tiles.shape[1]
    slots = seq_cos.shape[0] // base
    for i in range(slots):
        for j in range(slots):
            window = (pl.ds(i * base, base), pl.ds(j * base, base))
            number = numbers[i * slots + j]
            seq_cos[window] = cos_tiles[number]
            seq_sin[window] = sin_tiles[number]
    mix_forward(rows, hid_cos, hid_sin, seq_cos, seq_sin, gain, shift, real, imag, outs)


def expand_kernel(layer, n_sources, normed_low, b_in, *refs):
    sources, (hidden, hidden_turned, slope, scratch, sems) = refs[:n_sources], refs[n_sources:]
    width = scratch.shape[2]
    for chunk in Loader(layer, sources, scratch, sems, False):
        at_chunk = rows_at(chunk * width, width)

        @row_steps(normed_low.shape[0])
        def _(at):
            value, rate = gelu_both(dot(normed_low[at, :], scratch[chunk]) + b_in[:, at_chunk])
            value = value.astype(BF16)
            hidden[at, at_chunk] = value
            slope[at, at_chunk] = rate.astype(BF16)
            hidden_turned[at_chunk, at] = value.T


def contract(layer, sources, scratch, sems, hidden, total):
    width = scratch.shape[2]
    for turn, chunk in enumerate(Loader(layer, sources, scratch, sems, True)):
        at_chunk = rows_at(chunk * width, width)

        @row_steps(hidden.shape[0])
        def _(at):
            part = dot(hidden[at, at_chunk], scratch[chunk])
            total[at, :] = part if turn == 0 else total[at, :] + part


def middle_kernel(layer, n_sources, *refs):
    hidden, unit_one, gain_one, shift_one, b_out, gain_two, shift_two = refs[:7]
    hid_cos, hid_sin, seq_cos, seq_sin, next_gain, next_shift = refs[7:13]
    sources, refs = refs[13 : 13 + n_sources], refs[13 + n_sources :]
    unit_two, inverse_two = refs[:2]
    outs, (scratch, total, mid, real, imag, sems) = refs[2:6], refs[6:]
    contract(layer, sources, scratch, sems, hidden, total)

    @row_steps(hidden.shape[0])
    def _(at):
        normed = unit_one[at, :] * gain_one[...] + shift_one[...]
        unit, inverse = norm(normed + (total[at, :] + b_out[...]))
        unit_two[at, :] = unit
        inverse_two[at, :] = inverse
        mid[at, :] = (unit * gain_two[...] + shift_two[...]).astype(BF16)

    mix_forward(mid, hid_cos, hid_sin, seq_cos, seq_sin, next_gain, next_shift, real, imag, outs)


def out_grad(hidden_turned, branch_grad, tiles, storer):
    width = tiles.shape[2]
    for chunk in range(tiles.shape[0]):

        @row_steps(width)
        def _(at):
            rows = pl.ds(pl.multiple_of(chunk * width + at.start, at.size), at.size)
            tiles[chunk, at, :] = dot(hidden_turned[rows, :], branch_grad[...]).astype(BF16)

        storer.store(chunk)


def turn_kernel(layer, n_sources, n_outs, *refs):
    hidden, hidden_turned, unit_one, gain_one, shift_one, b_out, gain_two, shift_two = refs[:8]
    cotangent = refs[8]
    sources, refs = refs[9 : 9 + n_sources], refs[9 + n_sources :]
    grads, refs = refs[:n_outs], refs[n_outs:]
    out_rows, d_second, branch_grad, small = refs[:4]
    scratch, total, tiles, load_sems, store_sems = refs[4:]
    contract(layer, sources, scratch, load_sems, hidden, total)
    small[...] = jnp.zeros_like(small)

    @row_steps(hidden.shape[0])
    def _(at):
        normed = unit_one[at, :] * gain_one[...] + shift_one[...]
        unit, inverse = norm(normed + (total[at, :] + b_out[...]))
        out_rows[at, :] = unit * gain_two[...] + shift_two[...]
        second_back(at, cotangent[at, :].astype(F32), unit, inverse, gain_two, d_second, branch_grad, small)

    storer = Storer(grads, tiles, store_sems, True)
    out_grad(hidden_turned, branch_grad, tiles, storer)
    storer.finish()


def second_back(at, upstream, unit, inverse, gain, d_second, branch_grad, small):
    grad = norm_back(upstream, unit, inverse, gain[...])
    low = grad.astype(BF16)
    d_second[at, :] = grad
    branch_grad[at, :] = low
    small[0:1, :] += column_sum(low.astype(F32))
    small[1:2, :] += column_sum(upstream * unit)
    small[2:3, :] += column_sum(upstream)


def shrink_kernel(layer, n_sources, n_outs, branch_grad, slope, normed_turned, *refs):
    sources, refs = refs[:n_sources], refs[n_sources:]
    grads, refs = refs[:n_outs], refs[n_outs:]
    act_grad, b_grad = refs[:2]
    scratch, tiles, load_sems, store_sems = refs[2:]
    width = scratch.shape[2]
    b_grad[...] = jnp.zeros_like(b_grad)
    for chunk in Loader(layer, sources, scratch, load_sems, True):
        at_chunk = rows_at(chunk * width, width)

        @row_steps(branch_grad.shape[0])
        def _(at):
            grad = dot(branch_grad[at, :], scratch[chunk], ((1,), (1,)))
            low = (grad * slope[at, at_chunk].astype(F32)).astype(BF16)
            act_grad[at, at_chunk] = low
            b_grad[:, at_chunk] += column_sum(low.astype(F32))

    storer = Storer(grads, tiles, store_sems, False)
    for chunk in range(tiles.shape[0]):
        at_chunk = pl.ds(chunk * width, width)

        @row_steps(width)
        def _(at):
            tiles[chunk, at, :] = dot(normed_turned[at, :], act_grad[:, at_chunk]).astype(BF16)

        storer.store(chunk)
    storer.finish()


def unmix(layer, sources, scratch, sems, refs, small, input_grad):
    act_grad, d_second, unit_one, inverse_one, gain_one, hid_cos, hid_sin, seq_cos, seq_sin = refs[:9]
    total, mix_grad, real, imag = refs[9:]
    width = scratch.shape[2]
    for turn, chunk in enumerate(Loader(layer, sources, scratch, sems, False)):
        at_chunk = rows_at(chunk * width, width)

        @row_steps(act_grad.shape[0])
        def _(at):
            part = dot(act_grad[at, at_chunk], scratch[chunk], ((1,), (1,)))
            total[at, :] = (d_second if turn == 0 else total)[at, :] + part

    small[...] = jnp.zeros_like(small)

    @row_steps(act_grad.shape[0])
    def _(at):
        upstream, unit = total[at, :], unit_one[at, :]
        grad = norm_back(upstream, unit, inverse_one[at, :], gain_one[...])
        total[at, :] = grad
        mix_grad[at, :] = grad.astype(BF16)
        small[0:1, :] += column_sum(upstream * unit)
        small[1:2, :] += column_sum(upstream)

    @row_steps(act_grad.shape[0])
    def _(at):
        real[at, :] = dot(seq_cos[at, :], mix_grad[...]).astype(BF16)
        imag[at, :] = (-dot(seq_sin[at, :], mix_grad[...])).astype(BF16)

    @row_steps(act_grad.shape[0])
    def _(at):
        grad = dot(real[at, :], hid_cos[...]) + dot(imag[at, :], hid_sin[...])
        input_grad[at, :] = total[at, :] + grad


def last_kernel(layer, n_sources, *refs):
    sources, ins, (input_grad, small, scratch, total, mix_grad, real, imag, sems) = (
        refs[9 : 9 + n_sources],
        refs[:9],
        refs[9 + n_sources :],
    )
    unmix(layer, sources, scratch, sems, ins + (total, mix_grad, real, imag), small, input_grad)


def relay_kernel(layer, n_sources, n_outs, *refs):
    ins = refs[:9]
    hidden_turned, unit_two, inverse_two, gain_two = refs[9:13]
    sources, refs = refs[13 : 13 + n_sources], refs[13 + n_sources :]
    grads, refs = refs[:n_outs], refs[n_outs:]
    small, d_second, branch_grad, small_two = refs[:4]
    scratch, total, mix_grad, real, imag, tiles, load_sems, store_sems = refs[4:]
    unmix(layer, sources, scratch, load_sems, ins + (total, mix_grad, real, imag), small, total)
    small_two[...] = jnp.zeros_like(small_two)

    @row_steps(total.shape[0])
    def _(at):
        upstream = total[at, :].astype(BF16).astype(F32)
        second_back(
            at, upstream, unit_two[at, :], inverse_two[at, :], gain_two, d_second, branch_grad, small_two
        )

    storer = Storer(grads, tiles, store_sems, True)
    out_grad(hidden_turned, branch_grad, tiles, storer)
    storer.finish()


VMEM = pl.BlockSpec(memory_space=pltpu.VMEM)
SMEM = pl.BlockSpec(memory_space=pltpu.SMEM)
ANY = pl.BlockSpec(memory_space=pl.ANY)
SEMS = 40


def call(kernel, ins, outs, scratch, flops, name):
    sized = [pltpu.SemaphoreType.DMA((SEMS,)) if s is None else pltpu.VMEM(*s) for s in scratch]
    moved = sum(array.size * array.dtype.itemsize for _, array in ins)
    return pl.pallas_call(
        kernel,
        in_specs=[spec for spec, _ in ins],
        out_specs=tuple(spec for spec, _, _ in outs),
        out_shape=tuple(jax.ShapeDtypeStruct(shape, dtype) for _, shape, dtype in outs),
        scratch_shapes=sized,
        compiler_params=pltpu.CompilerParams(vmem_limit_bytes=48 * 2**20),
        cost_estimate=pl.CostEstimate(flops=flops, bytes_accessed=moved, transcendentals=0),
        name=name,
    )(*(array for _, array in ins))


def body(boundary, bucket_ids, w_in, b_in, w_out, b_out, gain_one, shift_one, gain_two, shift_two):
    place = Place()
    layers = w_in.shape[0]
    is_first = place.section % 2 == 0
    micro_count = bucket_ids.shape[1]
    feat_width = boundary.shape[2]
    slab_len = boundary.shape[1] // micro_count
    slots = bucket_ids.shape[2]
    base_len = slab_len // slots
    by_permutes = place.n_section == 4 and place.chips == 4

    def swap_layer(value):
        return place.permute(value, lambda s, z, c: (s ^ 1, z, c))

    first_slab, second_slab = boundary[0, :slab_len], boundary[0, slab_len:]
    received = swap_layer(jnp.where(is_first, second_slab, first_slab))
    rows = jnp.where(is_first, first_slab, received)
    cotangent = jnp.where(is_first, received, second_slab)
    bucket_row = bucket_ids[place.section // 2, place.section % 2]

    if by_permutes:
        others_in, others_out = place.swap_core(w_in), place.swap_core(w_out)
        sources_in, sources_out = [], []
        for layer in range(layers):
            for w, others, sources, by_rows in (
                (w_in, others_in, sources_in, False),
                (w_out, others_out, sources_out, True),
            ):
                near, far, other_near, other_far = gather_weight(place, w[layer], by_rows)
                sources.append([(ANY, v) for v in (w, near, far, others, other_near, other_far)])
    else:
        sources_in, sources_out = (
            [
                [(ANY, lax.all_gather(w[layer], "dp", axis=0, tiled=True))]
                for layer in range(layers)
            ]
            for w in (w_in, w_out)
        )

    ff_width = w_in.shape[2]
    chunks = ff_width // feat_width
    hid = [(VMEM, jnp.asarray(table.astype(BF16))) for table in dft_tables(feat_width)]
    numbers = tile_numbers(bucket_row, slots).reshape(-1)
    tiles = [(VMEM, jnp.asarray(table)) for table in sequence_tiles(base_len)]
    block = (slab_len, feat_width)
    wide = (slab_len, ff_width)
    square = 2 * slab_len * feat_width * feat_width
    mix_cost = 2 * square + 4 * slab_len * slab_len * feat_width
    ff_cost = 2 * slab_len * feat_width * ff_width
    loaded = ((chunks, feat_width, feat_width), BF16)
    sums_shape = (VMEM, (8, feat_width), F32)

    def vmem(*arrays):
        return [(VMEM, array) for array in arrays]

    def param(array, layer):
        return (VMEM, array[layer][None])

    mix_outs = [
        (VMEM, block, F32),
        (VMEM, (slab_len, 1), F32),
        (VMEM, block, BF16),
        (VMEM, (feat_width, slab_len), BF16),
    ]
    if by_permutes:
        pieces = {
            True: (4, place.chips, w_out.shape[1] // 4, feat_width),
            False: (4, place.chips, w_in.shape[1], feat_width),
        }
        grad_outs = {key: [(ANY, shape, BF16)] * 2 for key, shape in pieces.items()}
    else:
        grad_outs = {
            True: [(ANY, (ff_width, feat_width), BF16)],
            False: [(ANY, (feat_width, ff_width), BF16)],
        }
    n_sources, n_outs = len(sources_in[0]), len(grad_outs[True])

    seq_cos, seq_sin, *mixed = call(
        first_mix_kernel,
        [(SMEM, numbers), (VMEM, rows)] + hid + tiles + [param(gain_one, 0), param(shift_one, 0)],
        [(VMEM, (slab_len, slab_len), BF16)] * 2 + mix_outs,
        [(block, BF16)] * 2,
        mix_cost,
        "first_mix",
    )
    tables = hid + vmem(seq_cos, seq_sin)

    saved = []
    for layer in range(layers):
        unit_one, inverse_one, normed_low, normed_turned = mixed
        hidden, hidden_turned, slope = call(
            partial(expand_kernel, layer, n_sources),
            vmem(normed_low) + [param(b_in, layer)] + sources_in[layer],
            [(VMEM, wide, BF16), (VMEM, (ff_width, slab_len), BF16), (VMEM, wide, BF16)],
            [loaded, None],
            ff_cost,
            "expand",
        )
        common = vmem(unit_one) + [
            param(p, layer) for p in (gain_one, shift_one, b_out, gain_two, shift_two)
        ]
        kept = [unit_one, inverse_one, normed_turned, hidden_turned, slope]
        if layer < layers - 1:
            unit_two, inverse_two, *mixed = call(
                partial(middle_kernel, layer, n_sources),
                vmem(hidden)
                + common
                + tables
                + [param(gain_one, layer + 1), param(shift_one, layer + 1)]
                + sources_out[layer],
                [(VMEM, block, F32), (VMEM, (slab_len, 1), F32)] + mix_outs,
                [loaded, (block, F32), (block, BF16), (block, BF16), (block, BF16), None],
                ff_cost + mix_cost,
                "middle",
            )
            kept += [unit_two, inverse_two]
        saved.append(kept)

    last = layers - 1
    *pieces, out_rows, d_second, branch_grad, sums_two = call(
        partial(turn_kernel, last, n_sources, n_outs),
        vmem(hidden, hidden_turned) + common + vmem(cotangent) + sources_out[last],
        grad_outs[True]
        + [(VMEM, block, F32), (VMEM, block, F32), (VMEM, block, BF16), sums_shape],
        [loaded, (block, F32), loaded, None, None],
        2 * ff_cost,
        "turn",
    )
    grads_out, grads_in, smalls = {last: pieces}, {}, {}
    for layer in reversed(range(layers)):
        unit_one, inverse_one, normed_turned, hidden_turned, slope = saved[layer][:5]
        *pieces, act_grad, b_grad = call(
            partial(shrink_kernel, layer, n_sources, n_outs),
            vmem(branch_grad, slope, normed_turned) + sources_out[layer],
            grad_outs[False] + [(VMEM, wide, BF16), (VMEM, (1, ff_width), F32)],
            [loaded, loaded, None, None],
            2 * ff_cost,
            "shrink",
        )
        grads_in[layer] = pieces
        ins = vmem(act_grad, d_second, unit_one, inverse_one) + [param(gain_one, layer)] + tables
        own_sums = sums_two
        work = [loaded, (block, F32), (block, BF16), (block, BF16), (block, BF16)]
        if layer > 0:
            below_turned, below_unit, below_inverse = [saved[layer - 1][i] for i in (3, 5, 6)]
            *pieces, sums_one, d_second, branch_grad, sums_two = call(
                partial(relay_kernel, layer, n_sources, n_outs),
                ins
                + vmem(below_turned, below_unit, below_inverse)
                + [param(gain_two, layer - 1)]
                + sources_in[layer],
                grad_outs[True]
                + [sums_shape, (VMEM, block, F32), (VMEM, block, BF16), sums_shape],
                work + [loaded, None, None],
                2 * ff_cost + mix_cost,
                "relay",
            )
            grads_out[layer - 1] = pieces
        else:
            input_grad, sums_one = call(
                partial(last_kernel, layer, n_sources),
                ins + sources_in[layer],
                [(VMEM, block, F32), sums_shape],
                work + [None],
                ff_cost + mix_cost,
                "last",
            )
        smalls[layer] = (b_grad[0], own_sums[0], sums_one[0], sums_one[1], own_sums[1], own_sums[2])

    def reduce_grad(pieces, by_rows):
        if by_permutes:
            return share_sections(place, scatter_grad(place, *pieces), by_rows)
        part = lax.psum_scatter(pieces[0], "dp", scatter_dimension=0, tiled=True)
        return lax.psum(part, "section").astype(F32)

    grads = [
        (reduce_grad(grads_in[layer], False), reduce_grad(grads_out[layer], True))
        for layer in range(layers)
    ]

    stacked = [jnp.stack([smalls[layer][i] for layer in range(layers)]) for i in range(6)]
    widths = [value.shape[1] // place.n_dp for value in stacked]
    packed = jnp.concatenate(
        [value.reshape(layers, place.n_dp, -1).transpose(1, 0, 2) for value in stacked], axis=2
    )
    if by_permutes:
        own_small = sum_small(place, packed)
    else:
        own_small = lax.psum(
            lax.psum_scatter(packed, "dp", scatter_dimension=0, tiled=False), "section"
        )
    small_out, start = [], 0
    for width in widths:
        small_out.append(own_small[:, start : start + width])
        start += width

    sent = jnp.where(is_first, out_rows, input_grad).astype(BF16)
    back = swap_layer(sent).astype(F32)
    result = jnp.stack(
        [jnp.where(is_first, input_grad, back), jnp.where(is_first, back, out_rows)]
    ).reshape(1, micro_count * slab_len, feat_width)
    return (
        result,
        jnp.stack([grads[layer][0] for layer in range(layers)]),
        small_out[0],
        jnp.stack([grads[layer][1] for layer in range(layers)]),
        small_out[1],
        small_out[2],
        small_out[3],
        small_out[4],
        small_out[5],
    )


def solution(mesh):
    return jax.shard_map(
        body,
        mesh=mesh,
        in_specs=(
            P("section", "dp", None),
            P(None, "dp", None),
            P(None, "dp", None),
            P(),
            P(None, "dp", None),
            P(),
            P(),
            P(),
            P(),
            P(),
        ),
        out_specs=(
            P("section", "dp", None),
            P(None, "dp", None),
            P(None, "dp"),
            P(None, "dp", None),
            P(None, "dp"),
            P(None, "dp"),
            P(None, "dp"),
            P(None, "dp"),
            P(None, "dp"),
        ),
        check_vma=False,
    )
```

time: 1020 us -> 456 us (0.45)
  matrix products: 706 us -> 0 us
  Pallas kernels: 0 us -> 143 us
  starting transfers between devices: 6.48 us -> 86 us
  other arithmetic: 87.2 us -> 31.6 us
  blocking collectives: 38 us -> 0 us
  waiting for transfers between devices: 151 us -> 172 us
  between operations: 16.9 us -> 1.65 us
    dot_general x72 -> x0, matrix products: 706 us -> none  [the longest x7 110 us: forward_layer(): jnp.dot(seq_sin, imag_part, preferred_element_type=jnp.float32)]
    pallas_call x0 -> x9, Pallas kernels: none -> 143 us  [call(): pl.pallas_call(kernel, in_specs=[spec for spec, _ in ins], out_specs=tupl...]
    ppermute x3 -> x69, waiting for transfers between devices: 31.8 us -> 172 us  [permute(): return lax.ppermute(value, AXES, pairs)]
    reduce_scatter x2 -> x0, waiting for transfers between devices: 100 us -> none  [the longest x1 97.5 us: body(): lax.psum_scatter(grad_totals[0], 'dp', scatter_dimension=0, tiled=True)]
    ppermute x3 -> x69, starting transfers between devices: 6.28 us -> 86 us  [permute(): return lax.ppermute(value, AXES, pairs)]
    dot_general x2 -> x0, other arithmetic: 39.3 us -> none  [forward_layer(): jnp.dot(seq_cos, real_part, preferred_element_type=jnp.float32)]
    unnamed x1 -> x0, blocking collectives: 28.1 us -> none
    reduce_sum x43 -> x2, other arithmetic: 22.1 us -> 0.3 us  [the longest x1 0.18 us: tile_numbers(): size = jnp.sum(one_hot * parts[None, :], axis=1)]
  transfers between devices with their start and end apart: 8 -> 69, of which waited for: 6 -> 32; matrix products, arithmetic and copies ran while one was open for 27% -> 8% of each run, Pallas kernels for 0% -> 18%
where the time goes in v1:
time: 456 us; the launch traced here: 451 us
  waiting for transfers between devices  172 us (38%)
  Pallas kernels  143 us (31%)
  starting transfers between devices  86 us (19%)
  other arithmetic  31.6 us (7%)
  local copies, waits for them, and re-layouts  16.3 us (4%)
    ppermute x69, waiting for transfers between devices, permute(): return lax.ppermute(value, AXES, pairs)  172 us
    pallas_call x9, Pallas kernels, call(): pl.pallas_call(kernel, in_specs=[spec for spec, _ in ins], out_specs=tupl...  143 us
    ppermute x69, starting transfers between devices, permute(): return lax.ppermute(value, AXES, pairs)  86 us
    unnamed x88, local copies, waits for them, and re-layouts  10.3 us
  transfers between devices with their start and end apart: 69, of which 32 were waited for; matrix products, arithmetic and copies ran while one was open for 8% of the time, Pallas kernels for 18%

profile of v1, /device:TPU:0, one launch (start us, length us, event | category | flops | bytes accessed | tf_op | source)
XLA Modules:
  0.0 450.8 jit_solution(9803841645367825149)
XLA Ops:
  2.7 3.0 collective-permute-start.1
  16.8 7.1 %collective-permute-done.2 = bf16[96,768]{1,0:T(8,128)(2,1)} collective-permute-done((bf16[96,768]{1,0:T(8,128)(2,1)}, bf16[96,768]{1,0:T(8,128)(2,1)}, u32[]{:S(2)}, u32[]{:S(2)}) %collective-permute-start.2) | collective-permute-done | bytes 147488 | tf_op jit(solution)/shard_map/ppermute | solution.py:41
  23.9 3.6 collective-permute-start.17
  27.6 3.5 collective-permute-start.18
  32.8 3.4 collective-permute-done.10
  36.1 4.2 collective-permute-start.24
  42.9 3.4 collective-permute-start.25
  51.0 3.1 collective-permute-start.12
  63.6 7.2 %collective-permute-done.20 = bf16[3,96,768]{2,1,0:T(8,128)(2,1)S(1)} collective-permute-done((bf16[3,96,768]{2,1,0:T(8,128)(2,1)S(1)}, bf16[3,96,768]{2,1,0:T(8,128)(2,1)S(1)}, u32[]{:S(2)}, u32[]{:S(2)}) %collective-permute-start.20) | collective-permute-done | bytes 442400 | tf_op jit(solution)/shard_map/ppermute | solution.py:41
  72.2 8.3 %collective-permute-done.27 = bf16[3,96,768]{2,1,0:T(8,128)(2,1)} collective-permute-done((bf16[3,96,768]{2,1,0:T(8,128)(2,1)S(1)}, bf16[3,96,768]{2,1,0:T(8,128)(2,1)}, u32[]{:S(2)}, u32[]{:S(2)}) %collective-permute-start.27) | collective-permute-done | bytes 442400 | tf_op jit(solution)/shard_map/ppermute | solution.py:41
  81.7 15.5 %collective-permute-done = bf16[512,768]{1,0:T(8,128)(2,1)S(1)} collective-permute-done((bf16[512,768]{1,0:T(8,128)(2,1)S(1)}, bf16[512,768]{1,0:T(8,128)(2,1)S(1)}, u32[]{:S(2)}, u32[]{:S(2)}) %collective-permute-start) | collective-permute-done | bytes 786464 | tf_op jit(solution)/shard_map/ppermute | solution.py:41
  103.8 6.5 %collective-permute-done.13.refs_15_.refs_2_ = bf16[6,96,768]{2,1,0:T(8,128)(2,1)} collective-permute-done((bf16[6,96,768]{2,1,0:T(8,128)(2,1)S(1)}, bf16[6,96,768]{2,1,0:T(8,128)(2,1)}, u32[]{:S(2)}, u32[]{:S(2)}) %collective-permute-start.13) | collective-permute-done | bytes 884768 | tf_op jit(solution)/shard_map/ppermute | solution.py:41
  111.0 8.9 %collective-permute-done.21.refs_2_.refs_15_ = bf16[6,96,768]{2,1,0:T(8,128)(2,1)} collective-permute-done((bf16[6,96,768]{2,1,0:T(8,128)(2,1)}, bf16[6,96,768]{2,1,0:T(8,128)(2,1)}, u32[]{:S(2)}, u32[]{:S(2)}) %collective-permute-start.21) | collective-permute-done | bytes 884768 | tf_op jit(solution)/shard_map/ppermute | solution.py:41
  121.1 8.1 %collective-permute-done.28.refs_11_.refs_2_ = bf16[6,96,768]{2,1,0:T(8,128)(2,1)S(1)} collective-permute-done((bf16[6,96,768]{2,1,0:T(8,128)(2,1)S(1)}, bf16[6,96,768]{2,1,0:T(8,128)(2,1)S(1)}, u32[]{:S(2)}, u32[]{:S(2)}) %collective-permute-start.28) | collective-permute-done | bytes 884768 | tf_op jit(solution)/shard_map/ppermute | solution.py:41
  129.7 6.5 %first_mix.1 = (bf16[512,512]{1,0:T(8,128)(2,1)S(1)}, bf16[512,512]{1,0:T(8,128)(2,1)S(1)}, f32[512,768]{1,0:T(8,128)}, f32[512,1]{1,0:T(8,128)S(1)}, bf16[512,7...) custom-call(s32[16]{0:T(128)S(1)} %select_n.304.numbers, bf16[512,768]{1,0:T(8,128)(2,1)S(1)} %get-tuple-element.112.rows, ...), custom_call_target="tpu_custom_call" | custom-call | flops 2013265920 | bytes 4593728 | tf_op jit(solution)/shard_map/first_mix/pallas_call | solution.py:552
  139.4 14.0 %expand.2 = (bf16[512,3072]{1,0:T(8,128)(2,1)}, bf16[3072,512]{1,0:T(8,128)(2,1)}, bf16[512,3072]{1,0:T(8,128)(2,1)}) custom-call(bf16[512,768]{1,0:T(8,128)(2,1)S(1)} %copy-done.14, f32[1,3072]{1,0:T(1,128)S(1)} %get-tuple-element.154.b_in, bf16[2,96,3072]{2,1,0:T(8,128)(2,1)S(1)} %copy-done, bf16[6,96,768]{2,1,0:T(8,128)(2,1)S(1)} %pad_maximum_fusion.1.refs_1_.refs_10_, ...), custom_call_target="tpu_custom_call" | custom-call | flops 2415919104 | bytes 6696960 | tf_op jit(solution)/shard_map/expand/pallas_call | solution.py:552
  155.4 14.2 %middle.1 = (f32[512,768]{1,0:T(8,128)}, f32[512,1]{1,0:T(8,128)S(1)}, f32[512,768]{1,0:T(8,128)}, f32[512,1]{1,0:T(8,128)S(1)}, bf16[512,768]{1,0:T(8,128)(2,1)S(1)}, /*index=5*/bf16[768,512]{1,0:T(8,128)(2,1)S(1)}) custom-call(bf16[512,3072]{1,0:T(8,128)(2,1)} %get-tuple-element.50.refs_0_, f32[512,768]{1,0:T(8,128)} %get-tuple-element.51.refs_1_.refs_2_, ...), custom_call_target="tpu_custom_call" | custom-call | flops 4429185024 | bytes 14046208 | tf_op jit(solution)/shard_map/middle/pallas_call | solution.py:552
  169.7 13.8 %expand.3 = (bf16[512,3072]{1,0:T(8,128)(2,1)}, bf16[3072,512]{1,0:T(8,128)(2,1)}, bf16[512,3072]{1,0:T(8,128)(2,1)}) custom-call(bf16[512,768]{1,0:T(8,128)(2,1)S(1)} %get-tuple-element.54.normed_low, f32[1,3072]{1,0:T(1,128)S(1)} %get-tuple-element.153.b_in, bf16[2,96,3072]{2,1,0:T(8,128)(2,1)S(1)} %copy-done, ...), custom_call_target="tpu_custom_call" | custom-call | flops 2415919104 | bytes 6696960 | tf_op jit(solution)/shard_map/expand/pallas_call | solution.py:552
  183.5 20.4 %turn.1 = (bf16[4,4,96,768]{3,2,1,0:T(8,128)(2,1)}, bf16[4,4,96,768]{3,2,1,0:T(8,128)(2,1)}, f32[512,768]{1,0:T(8,128)}, f32[512,768]{1,0:T(8,128)}, bf16[512,768]{1,0:T(8,128)(2,1)S(1)}, /*index=5*/f32[8,768]{1,0:T(8,128)S(1)}) custom-call(bf16[512,3072]{1,0:T(8,128)(2,1)} %get-tuple-element.55.refs_0_, bf16[3072,512]{1,0:T(8,128)(2,1)} %get-tuple-element.56.refs_1_, ...), custom_call_target="tpu_custom_call" | custom-call | flops 4831838208 | bytes 14564352 | tf_op jit(solution)/shard_map/turn/pallas_call | solution.py:552
  203.8 17.8 %shrink.2 = (bf16[4,4,96,768]{3,2,1,0:T(8,128)(2,1)}, bf16[4,4,96,768]{3,2,1,0:T(8,128)(2,1)}, bf16[512,3072]{1,0:T(8,128)(2,1)}, f32[1,3072]{1,0:T(1,128)S(1)}) custom-call(bf16[512,768]{1,0:T(8,128)(2,1)S(1)} %get-tuple-element.58.branch_grad, bf16[512,3072]{1,0:T(8,128)(2,1)} %get-tuple-element.59.slope, ...), custom_call_target="tpu_custom_call" | custom-call | flops 4831838208 | bytes 10616832 | tf_op jit(solution)/shard_map/shrink/pallas_call | solution.py:552
  221.7 24.3 %relay.1 = (bf16[4,4,96,768]{3,2,1,0:T(8,128)(2,1)}, bf16[4,4,96,768]{3,2,1,0:T(8,128)(2,1)}, f32[8,768]{1,0:T(8,128)S(1)}, f32[512,768]{1,0:T(8,128)}, bf16[512...) custom-call(bf16[512,3072]{1,0:T(8,128)(2,1)} %get-tuple-element.61.refs_0_, f32[512,768]{1,0:T(8,128)} %get-tuple-element.62.refs_1_, ...), custom_call_target="tpu_custom_call" | custom-call | flops 6845104128 | bytes 20326400 | tf_op jit(solution)/shard_map/relay/pallas_call | solution.py:552
  251.0 16.8 %shrink.3 = (bf16[4,4,96,768]{3,2,1,0:T(8,128)(2,1)}, bf16[4,4,96,768]{3,2,1,0:T(8,128)(2,1)}, bf16[512,3072]{1,0:T(8,128)(2,1)}, f32[1,3072]{1,0:T(1,128)S(1)}) custom-call(bf16[512,768]{1,0:T(8,128)(2,1)S(1)} %copy-done.18, bf16[512,3072]{1,0:T(8,128)(2,1)} %get-tuple-element.68.slope, bf16[768,512]{1,0:T(8,128)(2,1)S(1)} %copy-done.16, ...), custom_call_target="tpu_custom_call" | custom-call | flops 4831838208 | bytes 10616832 | tf_op jit(solution)/shard_map/shrink/pallas_call | solution.py:552
  268.3 15.5 %last.1 = (f32[512,768]{1,0:T(8,128)}, f32[8,768]{1,0:T(8,128)S(1)}) custom-call(bf16[512,3072]{1,0:T(8,128)(2,1)} %get-tuple-element.70.refs_0_, f32[512,768]{1,0:T(8,128)} %get-tuple-element.71.refs_1_, f32[512,768]{1,0:T(8,128)} %get-tuple-element.51.refs_1_.refs_2_, f32[512,1]{1,0:T(8,128)S(1)} %copy-done.12, ...), custom_call_target="tpu_custom_call" | custom-call | flops 4429185024 | bytes 15602688 | tf_op jit(solution)/shard_map/last/pallas_call | solution.py:552
  284.8 3.7 collective-permute-done.48
  323.7 19.0 %collective-permute-done.54 = bf16[2,4,96,768]{3,2,1,0:T(8,128)(2,1)S(1)} collective-permute-done((bf16[2,4,96,768]{3,2,1,0:T(8,128)(2,1)S(1)}, bf16[2,4,96,768]{3,2,1,0:T(8,128)(2,1)S(1)}, u32[]{:S(2)}, u32[]{:S(2)}) %collective-permute-start.54) | collective-permute-done | bytes 1179680 | tf_op jit(solution)/shard_map/ppermute | solution.py:41
  345.2 20.5 %collective-permute-done.62 = bf16[2,4,96,768]{3,2,1,0:T(8,128)(2,1)S(1)} collective-permute-done((bf16[2,4,96,768]{3,2,1,0:T(8,128)(2,1)S(1)}, bf16[2,4,96,768]{3,2,1,0:T(8,128)(2,1)S(1)}, u32[]{:S(2)}, u32[]{:S(2)}) %collective-permute-start.62) | collective-permute-done | bytes 1179680 | tf_op jit(solution)/shard_map/ppermute | solution.py:41
  368.4 16.4 %collective-permute-done.33 = bf16[2,4,96,768]{3,2,1,0:T(8,128)(2,1)S(1)} collective-permute-done((bf16[2,4,96,768]{3,2,1,0:T(8,128)(2,1)S(1)}, bf16[2,4,96,768]{3,2,1,0:T(8,128)(2,1)S(1)}, u32[]{:S(2)}, u32[]{:S(2)}) %collective-permute-start.33) | collective-permute-done | bytes 1179680 | tf_op jit(solution)/shard_map/ppermute | solution.py:41
  387.3 10.0 %collective-permute-done.41 = bf16[2,4,96,768]{3,2,1,0:T(8,128)(2,1)S(1)} collective-permute-done((bf16[2,4,96,768]{3,2,1,0:T(8,128)(2,1)S(1)}, bf16[2,4,96,768]{3,2,1,0:T(8,128)(2,1)S(1)}, u32[]{:S(2)}, u32[]{:S(2)}) %collective-permute-start.41) | collective-permute-done | bytes 1179680 | tf_op jit(solution)/shard_map/ppermute | solution.py:41
  413.0 3.1 collective-permute-start.66
  428.7 3.0 collective-permute-done.44
  439.4 3.1 collective-permute-done.68
  445.7 3.1 collective-permute-done.47
  (292 shorter events, 138.0 us)
Async XLA Ops:
  8.3 19.3 %collective-permute-start.3 = (bf16[96,768]{1,0:T(8,128)(2,1)}, bf16[96,768]{1,0:T(8,128)(2,1)}, u32[]{:S(2)}, u32[]{:S(2)}) collective-permute-start(bf16[96,768]{1,0:T(8,128)(2,1)} %dynamic-slice_bitcast_fusion.3), channel_id=1, source_target_pairs={{0,6},{1,7},{2,0},{3,1},{4,2},{5,3},{6,4},{7,5},{8,14},{9,15},{10,... | collective-permute-start | bytes 442376 | tf_op jit(solution)/shard_map/ppermute | solution.py:41
  11.6 19.5 %collective-permute-start.9 = (bf16[96,768]{1,0:T(8,128)(2,1)}, bf16[96,768]{1,0:T(8,128)(2,1)S(1)}, u32[]{:S(2)}, u32[]{:S(2)}) collective-permute-start(bf16[96,768]{1,0:T(8,128)(2,1)} %dynamic-slice_bitcast_fusion.2), channel_id=1, source_target_pairs={{0,2},{1,3},{2,4},{3,5},{4,6},{5,7},{6,0},{7,1},{8,10},{9,11},{10,... | collective-permute-start | bytes 442376 | tf_op jit(solution)/shard_map/ppermute | solution.py:41
  12.3 23.8 %collective-permute-start.10 = (bf16[96,768]{1,0:T(8,128)(2,1)}, bf16[96,768]{1,0:T(8,128)(2,1)}, u32[]{:S(2)}, u32[]{:S(2)}) collective-permute-start(bf16[96,768]{1,0:T(8,128)(2,1)} %dynamic-slice_bitcast_fusion.2), channel_id=1, source_target_pairs={{0,4},{1,5},{2,6},{3,7},{4,0},{5,1},{6,2},{7,3},{8,12},{9,13},{10,... | collective-permute-start | bytes 442376 | tf_op jit(solution)/shard_map/ppermute | solution.py:41
  13.8 26.6 %collective-permute-start.11 = (bf16[96,768]{1,0:T(8,128)(2,1)}, bf16[96,768]{1,0:T(8,128)(2,1)S(1)}, u32[]{:S(2)}, u32[]{:S(2)}) collective-permute-start(bf16[96,768]{1,0:T(8,128)(2,1)} %dynamic-slice_bitcast_fusion.2), channel_id=1, source_target_pairs={{0,6},{1,7},{2,0},{3,1},{4,2},{5,3},{6,4},{7,5},{8,14},{9,15},{10,... | collective-permute-start | bytes 442376 | tf_op jit(solution)/shard_map/ppermute | solution.py:41
  27.6 21.6 %collective-permute-start.18 = (bf16[96,768]{1,0:T(8,128)(2,1)S(1)}, bf16[96,768]{1,0:T(8,128)(2,1)S(1)}, u32[]{:S(2)}, u32[]{:S(2)}) collective-permute-start(bf16[96,768]{1,0:T(8,128)(2,1)S(1)} %dynamic-slice_bitcast_fusion.1), channel_id=1, source_target_pairs={{0,4},{1,5},{2,6},{3,7},{4,0},{5,1},{6,2},{7,3},{8,12},{9,13},{10,... | collective-permute-start | bytes 442376 | tf_op jit(solution)/shard_map/ppermute | solution.py:41
  31.1 19.9 %collective-permute-start.19 = (bf16[96,768]{1,0:T(8,128)(2,1)S(1)}, bf16[96,768]{1,0:T(8,128)(2,1)S(1)}, u32[]{:S(2)}, u32[]{:S(2)}) collective-permute-start(bf16[96,768]{1,0:T(8,128)(2,1)S(1)} %dynamic-slice_bitcast_fusion.1), channel_id=1, source_target_pairs={{0,6},{1,7},{2,0},{3,1},{4,2},{5,3},{6,4},{7,5},{8,14},{9,15},{10,... | collective-permute-start | bytes 442376 | tf_op jit(solution)/shard_map/ppermute | solution.py:41
  40.4 19.0 %collective-permute-start.4 = (bf16[3,96,768]{2,1,0:T(8,128)(2,1)S(1)}, bf16[3,96,768]{2,1,0:T(8,128)(2,1)S(1)}, u32[]{:S(2)}, u32[]{:S(2)}) collective-permute-start(bf16[3,96,768]{2,1,0:T(8,128)(2,1)S(1)} %pad_maximum_fusion.5), channel_id=1, source_target_pairs={{0,8},{1,17},{2,10},{3,19},{4,12},{5,21},{6,14},{7,23},{8,0},{9,25... | collective-permute-start | bytes 1327112 | tf_op jit(solution)/shard_map/ppermute | solution.py:41
  54.3 45.3 %collective-permute-start.6 = (bf16[2,96,3072]{2,1,0:T(8,128)(2,1)S(1)}, bf16[2,96,3072]{2,1,0:T(8,128)(2,1)S(1)}, u32[]{:S(2)}, u32[]{:S(2)}) collective-permute-start(bf16[2,96,3072]{2,1,0:T(8,128)(2,1)S(1)} %copy-done), channel_id=1, source_target_pairs={{0,1},{1,0},{2,3},{3,2},{4,5},{5,4},{6,7},{7,6},{8,9},{9,8},{10,11... | collective-permute-start | bytes 3538952 | tf_op jit(solution)/shard_map/ppermute | solution.py:41
  56.3 43.3 %collective-permute-start.14 = (bf16[2,384,768]{2,1,0:T(8,128)(2,1)}, bf16[2,384,768]{2,1,0:T(8,128)(2,1)S(1)}, u32[]{:S(2)}, u32[]{:S(2)}) collective-permute-start(bf16[2,384,768]{2,1,0:T(8,128)(2,1)} %refs_0_.7), channel_id=1, source_target_pairs={{0,1},{1,0},{2,3},{3,2},{4,5},{5,4},{6,7},{7,6},{8,9},{9,8},{10,11... | collective-permute-start | bytes 3538952 | tf_op jit(solution)/shard_map/ppermute | solution.py:41
  59.4 21.0 %collective-permute-start.27 = (bf16[3,96,768]{2,1,0:T(8,128)(2,1)S(1)}, bf16[3,96,768]{2,1,0:T(8,128)(2,1)}, u32[]{:S(2)}, u32[]{:S(2)}) collective-permute-start(bf16[3,96,768]{2,1,0:T(8,128)(2,1)S(1)} %pad_maximum_fusion.8), channel_id=1, source_target_pairs={{0,8},{1,17},{2,10},{3,19},{4,12},{5,21},{6,14},{7,23},{8,0},{9,25... | collective-permute-start | bytes 1327112 | tf_op jit(solution)/shard_map/ppermute | solution.py:41
  60.4 36.8 %collective-permute-start = (bf16[512,768]{1,0:T(8,128)(2,1)S(1)}, bf16[512,768]{1,0:T(8,128)(2,1)S(1)}, u32[]{:S(2)}, u32[]{:S(2)}) collective-permute-start(bf16[512,768]{1,0:T(8,128)(2,1)S(1)} %copy-done.27), channel_id=1, source_target_pairs={{0,8},{1,9},{2,10},{3,11},{4,12},{5,13},{6,14},{7,15},{8,0},{9,1},... | collective-permute-start | bytes 2359304 | tf_op jit(solution)/shard_map/ppermute | solution.py:41
  70.9 31.6 %collective-permute-start.5 = (bf16[6,96,768]{2,1,0:T(8,128)(2,1)S(1)}, bf16[6,96,768]{2,1,0:T(8,128)(2,1)}, u32[]{:S(2)}, u32[]{:S(2)}) collective-permute-start(bf16[6,96,768]{2,1,0:T(8,128)(2,1)S(1)} %pad_maximum_fusion.1.refs_1_.refs_10_), channel_id=1, source_target_pairs={{0,16},{1,9},{2,18},{3,11},{4,20},{5,13},{6,22},{7,15},{8,24},{9,1... | collective-permute-start | bytes 2654216 | tf_op jit(solution)/shard_map/ppermute | solution.py:41
  80.4 22.7 %collective-permute-start.7 = (bf16[6,96,768]{2,1,0:T(8,128)(2,1)S(1)}, bf16[6,96,768]{2,1,0:T(8,128)(2,1)}, u32[]{:S(2)}, u32[]{:S(2)}) collective-permute-start(bf16[6,96,768]{2,1,0:T(8,128)(2,1)S(1)} %pad_maximum_fusion.1.refs_1_.refs_10_), channel_id=1, source_target_pairs={{0,1},{1,0},{2,3},{3,2},{4,5},{5,4},{6,7},{7,6},{8,9},{9,8},{10,11... | collective-permute-start | bytes 2654216 | tf_op jit(solution)/shard_map/ppermute | solution.py:41
  99.6 20.3 %collective-permute-start.21 = (bf16[6,96,768]{2,1,0:T(8,128)(2,1)}, bf16[6,96,768]{2,1,0:T(8,128)(2,1)}, u32[]{:S(2)}, u32[]{:S(2)}) collective-permute-start(bf16[6,96,768]{2,1,0:T(8,128)(2,1)} %pad_maximum_fusion.3.refs_1_.refs_14_), channel_id=1, source_target_pairs={{0,16},{1,9},{2,18},{3,11},{4,20},{5,13},{6,22},{7,15},{8,24},{9,1... | collective-permute-start | bytes 2654216 | tf_op jit(solution)/shard_map/ppermute | solution.py:41
  102.4 26.8 %collective-permute-start.28 = (bf16[6,96,768]{2,1,0:T(8,128)(2,1)S(1)}, bf16[6,96,768]{2,1,0:T(8,128)(2,1)S(1)}, u32[]{:S(2)}, u32[]{:S(2)}) collective-permute-start(bf16[6,96,768]{2,1,0:T(8,128)(2,1)S(1)} %pad_maximum_fusion.4.refs_10_.refs_1_), channel_id=1, source_target_pairs={{0,16},{1,9},{2,18},{3,11},{4,20},{5,13},{6,22},{7,15},{8,24},{9,1... | collective-permute-start | bytes 2654216 | tf_op jit(solution)/shard_map/ppermute | solution.py:41
  103.2 26.0 %collective-permute-start.8 = (bf16[6,96,768]{2,1,0:T(8,128)(2,1)}, bf16[6,96,768]{2,1,0:T(8,128)(2,1)S(1)}, u32[]{:S(2)}, u32[]{:S(2)}) collective-permute-start(bf16[6,96,768]{2,1,0:T(8,128)(2,1)} %collective-permute-done.5.refs_2_.refs_11_), channel_id=1, source_target_pairs={{0,1},{1,0},{2,3},{3,2},{4,5},{5,4},{6,7},{7,6},{8,9},{9,8},{10,11... | collective-permute-start | bytes 2654216 | tf_op jit(solution)/shard_map/ppermute | solution.py:41
  110.3 43.1 %collective-permute-start.16 = (bf16[6,96,768]{2,1,0:T(8,128)(2,1)}, bf16[6,96,768]{2,1,0:T(8,128)(2,1)S(1)}, u32[]{:S(2)}, u32[]{:S(2)}) collective-permute-start(bf16[6,96,768]{2,1,0:T(8,128)(2,1)} %collective-permute-done.13.refs_15_.refs_2_), channel_id=1, source_target_pairs={{0,1},{1,0},{2,3},{3,2},{4,5},{5,4},{6,7},{7,6},{8,9},{9,8},{10,11... | collective-permute-start | bytes 2654216 | tf_op jit(solution)/shard_map/ppermute | solution.py:41
  110.4 59.2 %collective-permute-start.22 = (bf16[6,96,768]{2,1,0:T(8,128)(2,1)}, bf16[6,96,768]{2,1,0:T(8,128)(2,1)S(1)}, u32[]{:S(2)}, u32[]{:S(2)}) collective-permute-start(bf16[6,96,768]{2,1,0:T(8,128)(2,1)} %pad_maximum_fusion.3.refs_1_.refs_14_), channel_id=1, source_target_pairs={{0,1},{1,0},{2,3},{3,2},{4,5},{5,4},{6,7},{7,6},{8,9},{9,8},{10,11... | collective-permute-start | bytes 2654216 | tf_op jit(solution)/shard_map/ppermute | solution.py:41
  119.8 49.8 %collective-permute-start.23 = (bf16[6,96,768]{2,1,0:T(8,128)(2,1)}, bf16[6,96,768]{2,1,0:T(8,128)(2,1)S(1)}, u32[]{:S(2)}, u32[]{:S(2)}) collective-permute-start(bf16[6,96,768]{2,1,0:T(8,128)(2,1)} %collective-permute-done.21.refs_2_.refs_15_), channel_id=1, source_target_pairs={{0,1},{1,0},{2,3},{3,2},{4,5},{5,4},{6,7},{7,6},{8,9},{9,8},{10,11... | collective-permute-start | bytes 2654216 | tf_op jit(solution)/shard_map/ppermute | solution.py:41
  129.2 54.3 %collective-permute-start.29 = (bf16[6,96,768]{2,1,0:T(8,128)(2,1)S(1)}, bf16[6,96,768]{2,1,0:T(8,128)(2,1)S(1)}, u32[]{:S(2)}, u32[]{:S(2)}) collective-permute-start(bf16[6,96,768]{2,1,0:T(8,128)(2,1)S(1)} %pad_maximum_fusion.4.refs_10_.refs_1_), channel_id=1, source_target_pairs={{0,1},{1,0},{2,3},{3,2},{4,5},{5,4},{6,7},{7,6},{8,9},{9,8},{10,11... | collective-permute-start | bytes 2654216 | tf_op jit(solution)/shard_map/ppermute | solution.py:41
  129.2 54.3 %collective-permute-start.30 = (bf16[6,96,768]{2,1,0:T(8,128)(2,1)S(1)}, bf16[6,96,768]{2,1,0:T(8,128)(2,1)}, u32[]{:S(2)}, u32[]{:S(2)}) collective-permute-start(bf16[6,96,768]{2,1,0:T(8,128)(2,1)S(1)} %collective-permute-done.28.refs_11_.refs_2_), channel_id=1, source_target_pairs={{0,1},{1,0},{2,3},{3,2},{4,5},{5,4},{6,7},{7,6},{8,9},{9,8},{10,11... | collective-permute-start | bytes 2654216 | tf_op jit(solution)/shard_map/ppermute | solution.py:41
  246.9 62.2 %collective-permute-start.53 = (bf16[4,4,96,768]{3,2,1,0:T(8,128)(2,1)}, bf16[4,4,96,768]{3,2,1,0:T(8,128)(2,1)}, u32[]{:S(2)}, u32[]{:S(2)}) collective-permute-start(bf16[4,4,96,768]{3,2,1,0:T(8,128)(2,1)} %get-tuple-element.86), channel_id=1, source_target_pairs={{0,1},{1,0},{2,3},{3,2},{4,5},{5,4},{6,7},{7,6},{8,9},{9,8},{10,11... | collective-permute-start | bytes 7077896 | tf_op jit(solution)/shard_map/ppermute | solution.py:41
  247.2 64.4 %collective-permute-start.61 = (bf16[4,4,96,768]{3,2,1,0:T(8,128)(2,1)}, bf16[4,4,96,768]{3,2,1,0:T(8,128)(2,1)}, u32[]{:S(2)}, u32[]{:S(2)}) collective-permute-start(bf16[4,4,96,768]{3,2,1,0:T(8,128)(2,1)} %get-tuple-element.88), channel_id=1, source_target_pairs={{0,1},{1,0},{2,3},{3,2},{4,5},{5,4},{6,7},{7,6},{8,9},{9,8},{10,11... | collective-permute-start | bytes 7077896 | tf_op jit(solution)/shard_map/ppermute | solution.py:41
  267.9 46.9 %collective-permute-start.32 = (bf16[4,4,96,768]{3,2,1,0:T(8,128)(2,1)}, bf16[4,4,96,768]{3,2,1,0:T(8,128)(2,1)}, u32[]{:S(2)}, u32[]{:S(2)}) collective-permute-start(bf16[4,4,96,768]{3,2,1,0:T(8,128)(2,1)} %get-tuple-element.76), channel_id=1, source_target_pairs={{0,1},{1,0},{2,3},{3,2},{4,5},{5,4},{6,7},{7,6},{8,9},{9,8},{10,11... | collective-permute-start | bytes 7077896 | tf_op jit(solution)/shard_map/ppermute | solution.py:41
  283.9 33.3 %collective-permute-start.40 = (bf16[4,4,96,768]{3,2,1,0:T(8,128)(2,1)}, bf16[4,4,96,768]{3,2,1,0:T(8,128)(2,1)S(1)}, u32[]{:S(2)}, u32[]{:S(2)}) collective-permute-start(bf16[4,4,96,768]{3,2,1,0:T(8,128)(2,1)} %get-tuple-element.78), channel_id=1, source_target_pairs={{0,1},{1,0},{2,3},{3,2},{4,5},{5,4},{6,7},{7,6},{8,9},{9,8},{10,11... | collective-permute-start | bytes 7077896 | tf_op jit(solution)/shard_map/ppermute | solution.py:41
  310.8 31.8 %collective-permute-start.54 = (bf16[2,4,96,768]{3,2,1,0:T(8,128)(2,1)S(1)}, bf16[2,4,96,768]{3,2,1,0:T(8,128)(2,1)S(1)}, u32[]{:S(2)}, u32[]{:S(2)}) collective-permute-start(bf16[2,4,96,768]{3,2,1,0:T(8,128)(2,1)S(1)} %add_convert_fusion.1), channel_id=1, source_target_pairs={{0,8},{1,17},{2,10},{3,19},{4,12},{5,21},{6,14},{7,23},{8,0},{9,25... | collective-permute-start | bytes 3538952 | tf_op jit(solution)/shard_map/ppermute | solution.py:41
  313.3 52.4 %collective-permute-start.62 = (bf16[2,4,96,768]{3,2,1,0:T(8,128)(2,1)S(1)}, bf16[2,4,96,768]{3,2,1,0:T(8,128)(2,1)S(1)}, u32[]{:S(2)}, u32[]{:S(2)}) collective-permute-start(bf16[2,4,96,768]{3,2,1,0:T(8,128)(2,1)S(1)} %add_convert_fusion), channel_id=1, source_target_pairs={{0,8},{1,17},{2,10},{3,19},{4,12},{5,21},{6,14},{7,23},{8,0},{9,25... | collective-permute-start | bytes 3538952 | tf_op jit(solution)/shard_map/ppermute | solution.py:41
  316.5 68.2 %collective-permute-start.33 = (bf16[2,4,96,768]{3,2,1,0:T(8,128)(2,1)S(1)}, bf16[2,4,96,768]{3,2,1,0:T(8,128)(2,1)S(1)}, u32[]{:S(2)}, u32[]{:S(2)}) collective-permute-start(bf16[2,4,96,768]{3,2,1,0:T(8,128)(2,1)S(1)} %add_convert_fusion.3), channel_id=1, source_target_pairs={{0,8},{1,17},{2,10},{3,19},{4,12},{5,21},{6,14},{7,23},{8,0},{9,25... | collective-permute-start | bytes 3538952 | tf_op jit(solution)/shard_map/ppermute | solution.py:41
  317.5 79.8 %collective-permute-start.41 = (bf16[2,4,96,768]{3,2,1,0:T(8,128)(2,1)S(1)}, bf16[2,4,96,768]{3,2,1,0:T(8,128)(2,1)S(1)}, u32[]{:S(2)}, u32[]{:S(2)}) collective-permute-start(bf16[2,4,96,768]{3,2,1,0:T(8,128)(2,1)S(1)} %add_convert_fusion.2), channel_id=1, source_target_pairs={{0,8},{1,17},{2,10},{3,19},{4,12},{5,21},{6,14},{7,23},{8,0},{9,25... | collective-permute-start | bytes 3538952 | tf_op jit(solution)/shard_map/ppermute | solution.py:41
  343.9 55.0 %collective-permute-start.55 = (bf16[4,96,768]{2,1,0:T(8,128)(2,1)S(1)}, bf16[4,96,768]{2,1,0:T(8,128)(2,1)S(1)}, u32[]{:S(2)}, u32[]{:S(2)}) collective-permute-start(bf16[4,96,768]{2,1,0:T(8,128)(2,1)S(1)} %fusion.4), channel_id=1, source_target_pairs={{0,16},{1,9},{2,18},{3,11},{4,20},{5,13},{6,22},{7,15},{8,24},{9,1... | collective-permute-start | bytes 1769480 | tf_op jit(solution)/shard_map/ppermute | solution.py:41
  367.0 36.6 %collective-permute-start.63 = (bf16[4,96,768]{2,1,0:T(8,128)(2,1)S(1)}, bf16[4,96,768]{2,1,0:T(8,128)(2,1)S(1)}, u32[]{:S(2)}, u32[]{:S(2)}) collective-permute-start(bf16[4,96,768]{2,1,0:T(8,128)(2,1)S(1)} %fusion.5), channel_id=1, source_target_pairs={{0,16},{1,9},{2,18},{3,11},{4,20},{5,13},{6,22},{7,15},{8,24},{9,1... | collective-permute-start | bytes 1769480 | tf_op jit(solution)/shard_map/ppermute | solution.py:41
  386.0 20.0 %collective-permute-start.34 = (bf16[4,96,768]{2,1,0:T(8,128)(2,1)S(1)}, bf16[4,96,768]{2,1,0:T(8,128)(2,1)S(1)}, u32[]{:S(2)}, u32[]{:S(2)}) collective-permute-start(bf16[4,96,768]{2,1,0:T(8,128)(2,1)S(1)} %fusion.2), channel_id=1, source_target_pairs={{0,16},{1,9},{2,18},{3,11},{4,20},{5,13},{6,22},{7,15},{8,24},{9,1... | collective-permute-start | bytes 1769480 | tf_op jit(solution)/shard_map/ppermute | solution.py:41
  (80 other events, 853.3 us)
